TPU v7x, 512 devices: a whole 4x8x8 slice. The times are simulated.
512 devices in a mesh: fsdp: 128 (over z, y, core), dp: 4 (over x).
Axes of the slice: x: 4, y: 8, z: 8, core: 2. Of those that a mesh axis runs over, the one named last changes fastest.
Arguments:
- tokens: bfloat16 [4, 512, 6144], P('dp', 'fsdp')
- act_cot: bfloat16 [4, 512, 12288], P('dp', None, 'fsdp')
- old_slots: bfloat16 [113255424], P('fsdp'), as said below
- offsets: int32 [129], replicated, may hold values from 0 to 75503616, as said below
Outputs:
- grad_shards: float32 [75503616], P('fsdp')
Inputs may be any that keep to these rules, and one draw needn't show every extreme that they name: offsets[0] is 0 and offsets[128] is 75503616; every offsets[i] lies within 147468 of i * 589872; one old range is exactly 884808 long in every draw. `old_slots`: slots past an owner's range hold arbitrary values.
All inputs are finite; a program needn't handle non-finite values.
Results may differ from a plain program's by a relative error of at most 0.0032.
The roundings to bfloat16 on the way count: a program that leaves them out, or rounds other values in their place, can miss the bound.
Values may be sent and summed in bfloat16 or wider, within the bound.
A program may use at most 64 MiB of HBM per device.

v0:
```python
import jax
import jax.numpy as jnp
from jax import lax
from jax.sharding import PartitionSpec as P

FLAT = 75503616


EPSILON = 1e-06


def padded(block, sides, width):
    for axis, dim in sides:
        count = lax.axis_size(axis)
        forward = [(i, i + 1) for i in range(count - 1)]
        backward = [(target, source) for source, target in forward]
        low = lax.ppermute(
            lax.slice_in_dim(block, block.shape[dim] - width, None, axis=dim), axis, forward
        )
        high = lax.ppermute(lax.slice_in_dim(block, 0, width, axis=dim), axis, backward)
        block = jnp.concatenate([low, block, high], axis=dim)
    return block


def body(tokens, act_cot, old_slots, offsets):
    owners = lax.axis_size("fsdp")
    my_rank = lax.axis_index("fsdp")
    width = tokens.shape[2]
    hid_dev = act_cot.shape[2]
    shard_len = FLAT // owners
    quarter = shard_len // 4
    gain_dev = width // owners
    range_start = lax.dynamic_index_in_dim(offsets, my_rank, 0, keepdims=False)
    range_end = lax.dynamic_index_in_dim(offsets, my_rank + 1, 0, keepdims=False)
    shift_low = range_start - my_rank * shard_len
    shift_high = range_end - (my_rank + 1) * shard_len
    range_len = range_end - range_start
    head_piece = old_slots[:quarter]
    tail_piece = lax.dynamic_slice_in_dim(old_slots, range_len - quarter, quarter, 0)
    edges = jnp.concatenate([head_piece, tail_piece])
    extended = padded(edges, (("fsdp", 0),), quarter)
    left_tail = extended[:quarter]
    right_head = extended[3 * quarter :]
    own_pad = jnp.concatenate(
        [jnp.zeros((quarter,), jnp.bfloat16), old_slots, jnp.zeros((quarter,), jnp.bfloat16)]
    )
    own_view = lax.dynamic_slice_in_dim(own_pad, quarter - shift_low, shard_len, 0)
    left_pad = jnp.concatenate([left_tail, jnp.zeros((shard_len + quarter,), jnp.bfloat16)])
    left_view = lax.dynamic_slice_in_dim(left_pad, quarter - shift_low, shard_len, 0)
    right_pad = jnp.concatenate(
        [
            jnp.zeros((shard_len + quarter,), jnp.bfloat16),
            right_head,
            jnp.zeros((quarter,), jnp.bfloat16),
        ]
    )
    right_view = lax.dynamic_slice_in_dim(right_pad, quarter - shift_high, shard_len, 0)
    positions = jnp.arange(shard_len, dtype=jnp.int32)
    shard = jnp.where(
        positions < shift_low,
        left_view,
        jnp.where(positions >= shard_len + shift_high, right_view, own_view),
    )
    w_block = shard[: hid_dev * width].reshape(hid_dev, width)
    gain_piece = shard[hid_dev * width :]
    norm_gain = lax.all_gather(gain_piece, "fsdp", axis=0, tiled=True)
    gain_float = norm_gain.astype(jnp.float32)
    cot_rows = act_cot[0]
    as_float = lax.all_gather(tokens, "fsdp", axis=1, tiled=True)[0].astype(jnp.float32)
    row_mean = jnp.mean(as_float, axis=-1, keepdims=True)
    centered = as_float - row_mean
    variance = jnp.mean(centered * centered, axis=-1, keepdims=True)
    normed = centered * lax.rsqrt(variance + EPSILON)
    scaled = (normed * gain_float).astype(jnp.bfloat16)
    pre_act = lax.dot_general(
        scaled, w_block, (((1,), (1,)), ((), ())), preferred_element_type=jnp.float32
    )
    cot_piece = cot_rows.astype(jnp.float32)
    _, gelu_back = jax.vjp(jax.nn.gelu, pre_act)
    pre_grad = gelu_back(cot_piece)[0].astype(jnp.bfloat16)
    grad_piece = lax.dot_general(
        pre_grad, scaled, (((0,), (0,)), ((), ())), preferred_element_type=jnp.float32
    )
    moment_piece = lax.dot_general(
        pre_grad.astype(jnp.float32),
        normed,
        (((0,), (0,)), ((), ())),
        precision=lax.Precision.HIGHEST,
        preferred_element_type=jnp.float32,
    )
    gain_part = jnp.sum(w_block.astype(jnp.float32) * moment_piece, axis=0)
    gain_total = lax.psum(gain_part, "fsdp")
    gain_mine = lax.dynamic_slice_in_dim(gain_total, my_rank * gain_dev, gain_dev, 0)
    combined = jnp.concatenate([grad_piece.reshape(-1), gain_mine])
    return lax.psum(combined, "dp")


def solution(mesh):
    placed = (P("dp", "fsdp", None), P("dp", None, "fsdp"), P("fsdp"), P())
    return jax.shard_map(body, mesh=mesh, in_specs=placed, out_specs=P("fsdp"), check_vma=False)
```

profile of v0, /device:TPU:1, one launch (start us, length us, event | category | flops | bytes accessed | tf_op | source)
XLA Modules:
  0.0 1177.0 jit_solution(14964635247262111271)
XLA Ops:
  6.5 1.5 copy.6
  8.1 0.0 all-gather.2.cloned.1.call-update
  8.1 0.0 all-reduce.4.cloned.1.call-start
  8.1 1.4 fusion.45
  10.8 2.0 fusion.44
  12.8 8.8 collective-permute-start.1
  21.6 1.9 collective-permute-start
  24.8 35.3 %concatenate.14 = bf16[1179744]{0:T(1024)(128)(2,1)} concatenate(bf16[147468]{0:T(1024)(128)(2,1)S(1)} %broadcast.54, bf16[884808]{0:T(1024)(128)(2,1)} %param.6, bf16[147468]{0:T(1024)(128)(2,1)S(1)} %broadcast.54), dimensions={0} | concatenate | bytes 4718976 | tf_op jit(solution)/shard_map/concatenate | solution.py:44
  60.2 1.3 dynamic-slice
  62.1 0.0 collective-permute-done.1
  62.2 0.7 copy-done.2
  62.9 0.1 broadcast.53
  63.0 16.4 %concatenate.13 = bf16[1032276]{0:T(1024)(128)(2,1)S(1)} concatenate(bf16[737340]{0:T(1024)(128)(2,1)S(1)} %broadcast.53, bf16[147468]{0:T(1024)(128)(2,1)} %copy-done.2, bf16[147468]{0:T(1024)(128)(2,1)} %copy-done), dimensions={0} | concatenate | bytes 4129104 | tf_op jit(solution)/shard_map/concatenate | solution.py:50
  79.4 3.3 fusion.24
  82.8 0.1 slice.13
  82.9 1.4 reshape.43
  84.2 0.2 dynamic-update-slice
  84.4 491.9 %all-reduce.1 = bf16[6144]{0:T(1024)(128)(2,1)S(1)} all-reduce(bf16[6144]{0:T(1024)(128)(2,1)S(1)} %dynamic-update-slice), channel_id=1, replica_groups=mesh['fsdp'=128,'dp'=4] {'fsdp'}, use_global_device_ids=true, to_apply=%add.1 | all-reduce | flops 6144 | bytes 24576
  576.3 9.5 convert_reduce_fusion
  585.8 0.0 copy-start.1
  585.8 0.0 copy-start.3
  585.9 1.8 fusion.10
  587.7 3.1 fusion.34
  590.8 6.6 fusion.29
  597.4 2.5 fusion.26
  599.9 0.4 copy.8
  600.4 490.9 %psum.14 = f32[6144]{0:T(1024)S(1)} all-reduce(f32[6144]{0:T(1024)S(1)} %fusion.29), channel_id=1, replica_groups=mesh['fsdp'=128,'dp'=4] {'fsdp'}, use_global_device_ids=true, to_apply=%region_3.4 | all-reduce | flops 6144 | bytes 49152 | tf_op jit(solution)/shard_map/psum | solution.py:92
  1091.2 0.1 dynamic_slice.28
  1091.3 1.6 pad_maximum_fusion
  1092.9 0.0 all-reduce.4.cloned.1.call-update
  1092.9 74.0 %all-reduce.4.cloned.1.call-done = f32[589872]{0:T(1024)} async-done(((f32[589872]{0:T(1024)}), f32[589872]{0:T(1024)}) %all-reduce.4.cloned.1.call-update) | async-done | bytes 2359504 | tf_op jit(solution)/shard_map/psum | solution.py:95
  1166.9 3.2 copy.12
  (14 shorter events, 0.1 us)
Async XLA Ops:
  6.5 569.7 %all-gather.2.cloned.1.call-start = ((), (), s32[]{:S(2)}) async-start(), calls=%async_computation | async-start | bytes 12681216 | tf_op jit(solution)/shard_map/all_gather | solution.py:69
  8.1 1158.9 %all-reduce.4.cloned.1.call-start = ((), (), s32[]{:S(2)}) async-start(), calls=%async_computation.1 | async-start | bytes 4726784 | tf_op jit(solution)/shard_map/psum | solution.py:95
  12.8 49.3 %collective-permute-start.1 = (bf16[147468]{0:T(1024)(128)(2,1)S(1)}, bf16[147468]{0:T(1024)(128)(2,1)S(1)}, u32[]{:S(2)}, u32[]{:S(2)}) collective-permute-start(bf16[147468]{0:T(1024)(128)(2,1)S(1)} %get-tuple-element.7), channel_id=1, source_target_pairs={{4,0},{8,4},{12,8},{16,12},{20,16},{24,20},{28,24},{32,28},{36,32}... | collective-permute-start | bytes 884816 | tf_op jit(solution)/shard_map/ppermute | solution.py:20
  21.6 57.8 %collective-permute-start = (bf16[147468]{0:T(1024)(128)(2,1)}, bf16[147468]{0:T(1024)(128)(2,1)}, u32[]{:S(2)}, u32[]{:S(2)}) collective-permute-start(bf16[147468]{0:T(1024)(128)(2,1)} %get-tuple-element.8), channel_id=1, source_target_pairs={{0,4},{4,8},{8,12},{12,16},{16,20},{20,24},{24,28},{28,32},{32,36}... | collective-permute-start | bytes 884816 | tf_op jit(solution)/shard_map/ppermute | solution.py:17
  24.8 37.3 %copy-start = (bf16[147468]{0:T(1024)(128)(2,1)}, bf16[147468]{0:T(1024)(128)(2,1)S(1)}, u32[]{:S(2)}) copy-start(bf16[147468]{0:T(1024)(128)(2,1)S(1)} %broadcast.54) | copy-start | bytes 884812
  62.1 0.7 copy-start.2
  585.8 1.8 copy-start.1
  585.8 1.8 copy-start.3
Sparse Core Ops, SparseCore 0:
  10.5 98.0 all-gather.1
  1093.0 73.8 all-reduce.3
where the time goes:
time: 1180 us
  blocking collectives  983 us (83%)
  waiting for transfers between devices  74.1 us (6%)
  local copies, waits for them, and re-layouts  64.2 us (5%)
  between operations  16.8 us (1%)
  other arithmetic  16.2 us (1%)
  matrix products  12.3 us (1%)
    unnamed x1, blocking collectives  492 us
    psum x1, blocking collectives, body(): gain_total = lax.psum(gain_part, 'fsdp')  491 us
    psum x1, waiting for transfers between devices, body(): return lax.psum(combined, 'dp')  74 us
    concatenate x1, local copies, waits for them, and re-layouts, body(): jnp.concatenate([jnp.zeros((quarter,), jnp.bfloat16), old_slots, jnp.zero...  35.3 us
  transfers between devices with their start and end apart: 4, of which 1 were waited for; matrix products, arithmetic and copies ran while one was open for 5% of the time, Pallas kernels for 0%

commit v1 on v0

v1 whole, which is shorter than its diff:
```python
import jax
import jax.numpy as jnp
import numpy as np
from jax import lax
from jax.experimental import pallas as pl
from jax.experimental.pallas import tpu as pltpu
from jax.sharding import PartitionSpec as P

D = 6144
HID_DEV = 96
SHARD = 589872
EPSILON = 1e-06
LINES = 6928
FRONT = 2704
BACK = 384
BLOCK = 768
LANES = 128
A_ROWS = 112
C_ROWS = 208
F32 = jnp.float32
BF16 = jnp.bfloat16


def lane_iota(rows):
    return lax.broadcasted_iota(jnp.int32, (rows, LANES), 1)


def three_terms(value):
    high = value.astype(BF16).astype(F32)
    rest = value - high
    mid = rest.astype(BF16).astype(F32)
    return high, mid, rest - mid


def prepare_kernel(tok_ref, slots_ref, off_ref, msg_ref, own_ref, right_ref, left_ref, wide, lines, packed):
    x = lax.axis_index("dp")
    j = lax.axis_index("fsdp")
    start = off_ref[j]
    length = off_ref[j + 1] - start
    shift_own = j * SHARD - start
    shift_right = shift_own + SHARD
    shift_left = shift_own - SHARD

    def widen(i, carry):
        rows = pl.ds(pl.multiple_of(i * 16, 16), 16)
        wide[pl.ds(pl.multiple_of(FRONT + i * 16, 16), 16), :] = slots_ref[rows, :].astype(F32)
        return carry

    lax.fori_loop(0, LINES // 16, widen, 0, unroll=8)

    def extract(first, shift, rows):
        turn = shift & (LANES - 1)
        at = FRONT + first + lax.shift_right_arithmetic(shift, 7)
        here = wide[pl.ds(at, rows), :]
        after = wide[pl.ds(at + 1, rows), :]
        back = (LANES - turn) & (LANES - 1)
        lane = lane_iota(rows)
        line = lax.broadcasted_iota(jnp.int32, (rows, LANES), 0)
        moved = jnp.where(lane < LANES - turn, pltpu.roll(here, back, 1), pltpu.roll(after, back, 1))
        slot = (first + line) * LANES + lane + shift
        return jnp.where((slot >= 0) & (slot < length), moved, 0.0)

    def piece(out_ref, first_row, rows, shift):
        def one(h, carry):
            got = extract((first_row + h) * 48 + 12 * x, shift, 16)
            lines[pl.ds(pl.multiple_of(h * 16, 16), 16), :] = got
            return carry

        lax.fori_loop(0, rows, one, 0, unroll=4)
        for k in range(12):
            col = lines[pl.ds(k, rows, stride=16), :]
            out_ref[k // 6, :, (k % 6) * LANES : (k % 6 + 1) * LANES] = col.astype(BF16)

    piece(own_ref, 0, 96, shift_own)
    piece(right_ref, 0, 32, shift_right)
    piece(left_ref, 64, 32, shift_left)

    lane8 = lane_iota(8)
    gain_own = extract(0, shift_own + HID_DEV * D - 16, 8)
    gain_left = extract(0, shift_left + HID_DEV * D - 64, 8)
    gains = jnp.where(
        (lane8 >= 16) & (lane8 < 64), gain_own, jnp.where((lane8 >= 64) & (lane8 < 112), gain_left, 0.0)
    )[0:1]

    tok = tok_ref[0].astype(F32)
    mean = jnp.mean(tok, axis=-1, keepdims=True)
    centered = tok - mean
    variance = jnp.mean(centered * centered, axis=-1, keepdims=True)
    scale = lax.rsqrt(variance + EPSILON)
    lane4 = lane_iota(4)
    extra = jnp.where((lane4 >= 16) & (lane4 < 112), jnp.broadcast_to(gains, (4, LANES)), 0.0)
    for n, term in enumerate(three_terms(mean) + three_terms(scale)):
        extra = jnp.where((lane4 == n) | (lane4 == n + 8), term, extra)
    for b in range(8):
        for k in range(6):
            col = (6 * b + k) * LANES
            packed[32 * b + 4 * k : 32 * b + 4 * k + 4, :] = tok[:, col : col + LANES]
        packed[32 * b + 24 : 32 * b + 28, :] = extra
        packed[32 * b + 28 : 32 * b + 32, :] = jnp.zeros((4, LANES), F32)
    for b in range(8):
        msg_ref[b] = packed[32 * b : 32 * b + 32, :].astype(BF16)


def gelu_slope(v):
    root = 0.7978845608028654
    t = jnp.tanh(root * (v + 0.044715 * (v * v * v)))
    return 0.5 * (1.0 + t) + 0.5 * v * (1.0 - t * t) * (root * (1.0 + 3 * 0.044715 * (v * v)))


def main_kernel(
    msg_ref, own_ref, right_ref, left_ref, cot_ref, pick_ref, mask_ref, out_ref,
    mail, edge_right, edge_left, weight, gath, norm, scaled, part, part_in, sums, sums_in,
    grads, result, spill, block_out, gain_rows, gain_mine, gain_z, gain_y, gain_out,
    mail_s, mail_r, edge_s, edge_r, core_s, core_r, one_s, one_r, two_s, two_r,
    sum_s, sum_r, pg_s, pg_r, res_s, res_r, gz_s, gz_r, gy_s, gy_r, gf_s, gf_r,
):
    x = lax.axis_index("dp")
    f = lax.axis_index("fsdp")
    c = f % 2
    y = (f // 2) % 8
    z = f // 16
    g = 2 * x + c
    other = 1 - c
    su = 2 + 14 * c
    sv = 16 - 14 * c
    pu = y + c * (z - y)
    pv = z + c * (y - z)
    sends = []

    def at(xx, ff):
        return {"dp": xx, "fsdp": ff}

    def mate(gg):
        return at(gg // 2, f - c + gg % 2)

    def dev_u(d):
        return at(x, ((pu + d + 8) % 8) * su + pv * sv + c)

    def dev_v(d):
        return at(x, pu * su + ((pv + d + 8) % 8) * sv + c)

    def dev_y(d):
        return at(x, z * 16 + ((y + d) % 8) * 2 + c)

    def dev_z(d):
        return at(x, ((z + d) % 8) * 16 + y * 2 + c)

    def dev_x(d):
        return at((x + d + 4) % 4, f)

    core = at(x, f - c + other)
    right = at(x, (f + 1) % 128)
    left = at(x, (f + 127) % 128)

    def copy(src, dst, ssem, rsem, dev):
        return pltpu.make_async_remote_copy(
            src_ref=src, dst_ref=dst, send_sem=ssem, recv_sem=rsem,
            device_id=dev, device_id_type=pl.DeviceIdType.MESH,
        )

    def send(src, dst, ssem, rsem, dev):
        one = copy(src, dst, ssem, rsem, dev)
        one.start()
        sends.append(one)

    def arrive(dst, ssem, rsem):
        copy(dst, dst, ssem, rsem, core).wait_recv()

    barrier = pltpu.get_barrier_semaphore()
    peers = [mate((g + r) % 8) for r in range(1, 8)]
    peers += [dev_y(r) for r in range(1, 8)] + [dev_z(r) for r in range(1, 8)] + [right, left]
    for dev in peers:
        pl.semaphore_signal(barrier, inc=1, device_id=dev, device_id_type=pl.DeviceIdType.MESH)
    pl.semaphore_wait(barrier, len(peers))

    for r in range(1, 8):
        gg = (g + r) % 8
        send(msg_ref.at[gg], mail.at[g], mail_s.at[r - 1], mail_r.at[r - 1], mate(gg))
    send(right_ref, edge_right, edge_s.at[0], edge_r.at[0], right)
    send(left_ref, edge_left, edge_s.at[1], edge_r.at[1], left)
    mail[pl.ds(g, 1)] = msg_ref[pl.ds(g, 1)]
    for r in range(1, 8):
        arrive(mail.at[(g - r + 8) % 8], mail_s.at[r - 1], mail_r.at[r - 1])

    letters = mail[...].reshape(256, LANES)
    out_row = lax.broadcasted_iota(jnp.int32, (C_ROWS, 256), 0)
    in_row = lax.broadcasted_iota(jnp.int32, (C_ROWS, 256), 1)
    token = out_row & 31
    want = 32 * (token >> 2) + 4 * (out_row >> 5) + (token & 3)
    chunk = jnp.dot((want == in_row).astype(BF16), letters, preferred_element_type=F32)
    out_row = lax.broadcasted_iota(jnp.int32, (16, 256), 0) + 16
    in_row = lax.broadcasted_iota(jnp.int32, (16, 256), 1)
    want = 32 * (out_row >> 2) + 24 + (out_row & 3)
    late = jnp.dot((want == in_row).astype(BF16), letters, preferred_element_type=F32)
    lane = lane_iota(16)
    extra = jnp.where((lane >= 8) & (lane < 16), late, chunk[192:208])
    gath[pu, pv, 0:192, :] = chunk[0:192].astype(BF16)
    gath[pu, pv, 192:208, :] = extra.astype(BF16)

    def first_a(i):
        return gath.at[i, pv, 0:A_ROWS]

    def first_b(i):
        return gath.at[pu, i, A_ROWS:C_ROWS]

    def second_a(h, i):
        return gath.at[4 * h : 4 * h + 4, i, 0:A_ROWS]

    def second_b(h, i):
        return gath.at[i, 4 * h : 4 * h + 4, A_ROWS:C_ROWS]

    streams = ((first_a, pu, dev_u, 1), (first_b, pv, dev_v, -1))
    for s in range(1, 5):
        for n, (slot, p, dev, full) in enumerate(streams):
            for m, d in enumerate((1, -1)):
                if s < 4 or d == full:
                    src = slot((p - d * (s - 1) + 8) % 8)
                    send(src, src, one_s.at[n, m, s - 1], one_r.at[n, m, s - 1], dev(d))
        for n, (slot, p, dev, full) in enumerate(streams):
            for m, d in enumerate((1, -1)):
                if s < 4 or d == full:
                    arrive(slot((p - d * s + 8) % 8), one_s.at[n, m, s - 1], one_r.at[n, m, s - 1])

    streams = ((second_a, pv, dev_v), (second_b, pu, dev_u))
    for s in range(1, 6):
        for h in range(2):
            for n, (slot, p, dev) in enumerate(streams):
                for m, d in enumerate((1, -1)):
                    if 1 < s and (s < 5 or h == m):
                        arrive(slot(h, (p - d * (s - 1) + 8) % 8), two_s.at[n, m, h, s - 2], two_r.at[n, m, h, s - 2])
                    if s < 4 or (s == 4 and h == m):
                        src = slot(h, (p - d * (s - 1) + 8) % 8)
                        send(src, src, two_s.at[n, m, h, s - 1], two_r.at[n, m, h, s - 1], dev(d))

        if s == 1:
            arrive(edge_right, edge_s.at[0], edge_r.at[0])
            arrive(edge_left, edge_s.at[1], edge_r.at[1])
            for half in range(2):
                spill[half, 0:32, :] = own_ref[half, 0:32, :] + edge_right[half]
                spill[half, 32:64, :] = own_ref[half, 32:64, :]
                spill[half, 64:96, :] = own_ref[half, 64:96, :] + edge_left[half]
            send(spill.at[other], weight.at[c], core_s.at[0], core_r.at[0], core)
            weight[pl.ds(c, 1)] = spill[pl.ds(c, 1)]
    arrive(weight.at[other], core_s.at[0], core_r.at[0])

    def chip(yy, zz):
        return yy + c * (zz - yy), zz + c * (yy - zz)

    for yy in range(9):
        uu, vv = chip(yy % 8, (g + yy // 8) % 8)
        rows = gath[uu, vv, 192:208, :].astype(F32)
        if yy < 8:
            gain_rows[2 * yy : 2 * yy + 1, :] = rows[0:1]
            gain_rows[2 * yy + 1 : 2 * yy + 2, :] = rows[4:5]
            gain_rows[16 + 2 * yy : 17 + 2 * yy, :] = rows[4:5]
        if yy > 0:
            gain_rows[15 + 2 * yy : 16 + 2 * yy, :] = rows[0:1]
    spread = jnp.dot(gain_rows[0:16, :].astype(BF16), pick_ref[0], preferred_element_type=F32)
    spread += jnp.dot(gain_rows[16:32, :].astype(BF16), pick_ref[1], preferred_element_type=F32)
    gain = jnp.sum(spread * mask_ref[...], axis=0, keepdims=True)

    def normalize(i, carry):
        zz = i // 4
        pair = i % 4
        data = []
        for side in range(2):
            uu, vv = chip(2 * pair + side, zz)
            rows = gath[uu, vv, 192:208, :].astype(F32)
            cols = []
            for base in (0, 3):
                early = (rows[:, base : base + 1] + rows[:, base + 1 : base + 2]) + rows[:, base + 2 : base + 3]
                late = (rows[:, base + 8 : base + 9] + rows[:, base + 9 : base + 10]) + rows[:, base + 10 : base + 11]
                cols.append((early[0:8], early[8:16], late[0:8], late[8:16]))
            data.append((uu, vv, cols))
        for k in range(6):
            gain_k = gain[:, k * LANES : (k + 1) * LANES]
            tiles = [gath[uu, vv, 32 * k : 32 * k + 32, :].astype(F32) for uu, vv, _ in data]
            for xx in range(4):
                both = jnp.concatenate(
                    [
                        (tiles[side][8 * xx : 8 * xx + 8] - data[side][2][0][xx]) * data[side][2][1][xx]
                        for side in range(2)
                    ],
                    axis=0,
                )
                rows = pl.ds(pl.multiple_of(512 * xx + 16 * i, 16), 16)
                norm[rows, k * LANES : (k + 1) * LANES] = both
                scaled[rows, k * LANES : (k + 1) * LANES] = (both * gain_k).astype(BF16)
        return carry

    lax.fori_loop(0, 32, normalize, 0)

    block = weight[...].reshape(192, BLOCK)
    for xx in range(4):
        for half in range(2):
            at_row = 512 * xx + 256 * half
            got = lax.dot_general(
                block, scaled[at_row : at_row + 256, :], (((1,), (1,)), ((), ())), preferred_element_type=F32
            )
            part[0, xx, :, 256 * half : 256 * half + 256] = got[0:96]
            part[1, xx, :, 256 * half : 256 * half + 256] = got[96:192]
    send(part.at[other], part_in, core_s.at[1], core_r.at[1], core)
    arrive(part_in, core_s.at[1], core_r.at[1])
    sums[...] = part[pl.ds(c, 1)][0] + part_in[...]
    for r in range(1, 4):
        send(sums.at[(x + r) % 4], sums_in.at[r - 1], sum_s.at[r - 1], sum_r.at[r - 1], dev_x(r))
    for r in range(1, 4):
        arrive(sums_in.at[r - 1], sum_s.at[r - 1], sum_r.at[r - 1])
    pre_act = (sums[pl.ds(x, 1)][0] + sums_in[0]) + (sums_in[1] + sums_in[2])
    pre_grad = (cot_ref[...].astype(F32) * gelu_slope(pre_act)).astype(BF16)

    mine = pl.ds(pl.multiple_of(96 * c, 32), 96)
    theirs = pl.ds(pl.multiple_of(96 * other, 32), 96)
    grads[pl.ds(x, 1), mine, :] = pre_grad[None]
    for r in range(1, 4):
        send(grads.at[x, mine], grads.at[x, mine], pg_s.at[r - 1], pg_r.at[r - 1], dev_x(r))
    for r in range(1, 4):
        arrive(grads.at[(x - r + 4) % 4, mine], pg_s.at[r - 1], pg_r.at[r - 1])
    send(grads.at[:, mine], grads.at[:, mine], core_s.at[2], core_r.at[2], core)
    arrive(grads.at[:, theirs], core_s.at[2], core_r.at[2])

    total = jnp.zeros((192, BLOCK), F32)
    for xx in range(4):
        total += jnp.dot(grads[xx], scaled[512 * xx : 512 * xx + 512, :], preferred_element_type=F32)
    rounded = total.astype(BF16)
    block_out[0] = rounded[0:96]
    block_out[1] = rounded[96:192]
    send(block_out.at[other], result.at[x, c], core_s.at[3], core_r.at[3], core)
    result[pl.ds(x, 1), pl.ds(c, 1)] = block_out[pl.ds(c, 1)][None]
    for m, d in enumerate((1, -1)):
        send(result.at[x, c], result.at[x, c], res_s.at[m, 0], res_r.at[m, 0], dev_x(d))
    arrive(result.at[x, other], core_s.at[3], core_r.at[3])
    for m, d in enumerate((1, -1)):
        send(result.at[x, other], result.at[x, other], res_s.at[m, 1], res_r.at[m, 1], dev_x(d))

    gain_sum = jnp.zeros((1, BLOCK), F32)
    for xx in range(4):
        for half in range(2):
            back = lax.dot_general(
                grads[xx, :, 256 * half : 256 * half + 256], block, (((0,), (0,)), ((), ())),
                preferred_element_type=F32,
            )
            at_row = 512 * xx + 256 * half
            gain_sum += jnp.sum(back * norm[at_row : at_row + 256, :], axis=0, keepdims=True)
    for k in range(6):
        gain_mine[k : k + 1, :] = gain_sum[:, k * LANES : (k + 1) * LANES]
    gain_mine[6:8, :] = jnp.zeros((2, LANES), F32)
    apart = (z - g + 8) % 8

    arrive(result.at[(x + 3) % 4, c], res_s.at[0, 0], res_r.at[0, 0])
    arrive(result.at[(x + 1) % 4, c], res_s.at[1, 0], res_r.at[1, 0])
    arrive(result.at[(x + 3) % 4, other], res_s.at[0, 1], res_r.at[0, 1])
    send(result.at[(x + 3) % 4, 0], result.at[(x + 3) % 4, 0], res_s.at[0, 2], res_r.at[0, 2], dev_x(1))
    arrive(result.at[(x + 1) % 4, other], res_s.at[1, 1], res_r.at[1, 1])
    send(result.at[(x + 1) % 4, 1], result.at[(x + 1) % 4, 1], res_s.at[1, 2], res_r.at[1, 2], dev_x(-1))

    @pl.when(apart != 0)
    def _():
        to_z = copy(
            gain_mine, gain_z.at[apart - 1], gz_s, gz_r.at[apart - 1], at(x, g * 16 + y * 2 + c)
        )
        to_z.start()
        to_z.wait_send()

    @pl.when(apart == 0)
    def _():
        sum_z = gain_mine[...]
        for r in range(7):
            arrive(gain_z.at[r], gz_s, gz_r.at[r])
            sum_z += gain_z[r]
        gain_y[7] = sum_z
        outs = [
            copy(gain_y.at[7], gain_y.at[r - 1], gy_s.at[r - 1], gy_r.at[r - 1], dev_y(r)) for r in range(1, 8)
        ]
        for one in outs:
            one.start()
        for r in range(7):
            arrive(gain_y.at[r], gy_s.at[r], gy_r.at[r])
            sum_z += gain_y[r]
        gain_out[...] = sum_z
        for one in outs:
            one.wait_send()
        outs = [copy(gain_out, gain_out, gf_s.at[r - 1], gf_r, mate((g + r) % 8)) for r in range(1, 8)]
        for one in outs:
            one.start()
        for one in outs:
            one.wait_send()

    @pl.when(apart != 0)
    def _():
        arrive(gain_out, gf_s.at[0], gf_r)

    first = 48 * (2 * y + c)
    turn = first % LANES
    line = first // LANES
    here = jnp.broadcast_to(gain_out[pl.ds(line, 1), :], (8, LANES))
    after = jnp.broadcast_to(gain_out[pl.ds(line + 1, 1), :], (8, LANES))
    back = (LANES - turn) % LANES
    moved = jnp.where(lane_iota(8) < LANES - turn, pltpu.roll(here, back, 1), pltpu.roll(after, back, 1))
    out_ref[4608:4616, :] = moved

    def spell(xx, half):
        for k in range(6):
            col = result[xx, half, :, k * LANES : (k + 1) * LANES].astype(F32)
            out_ref[pl.ds(12 * xx + 6 * half + k, 96, stride=48), :] = col

    arrive(result.at[(x + 2) % 4, 0], res_s.at[0, 2], res_r.at[0, 2])
    arrive(result.at[(x + 2) % 4, 1], res_s.at[1, 2], res_r.at[1, 2])
    for xx in range(4):
        for half in range(2):
            spell(xx, half)
    for one in sends:
        one.wait_send()


def body(tokens, act_cot, old_slots, offsets):
    vmem = pl.BlockSpec(memory_space=pltpu.VMEM)
    smem = pl.BlockSpec(memory_space=pltpu.SMEM)
    dma = pltpu.SemaphoreType.DMA
    slots = jnp.pad(old_slots, (0, LINES * LANES - old_slots.shape[0])).reshape(LINES, LANES)
    msg, own, right, left = pl.pallas_call(
        prepare_kernel,
        out_shape=[
            jax.ShapeDtypeStruct((8, 32, LANES), BF16),
            jax.ShapeDtypeStruct((2, 96, BLOCK), BF16),
            jax.ShapeDtypeStruct((2, 32, BLOCK), BF16),
            jax.ShapeDtypeStruct((2, 32, BLOCK), BF16),
        ],
        in_specs=[vmem, vmem, smem],
        out_specs=[vmem] * 4,
        scratch_shapes=[
            pltpu.VMEM((FRONT + LINES + BACK, LANES), F32),
            pltpu.VMEM((96 * 16, LANES), F32),
            pltpu.VMEM((256, LANES), F32),
        ],
        compiler_params=pltpu.CompilerParams(vmem_limit_bytes=24 * 2**20),
    )(tokens, slots, offsets)

    n = np.arange(BLOCK)
    lanes = np.arange(LANES)[:, None]
    pick = jnp.asarray(np.stack([lanes == 16 + n % 48, lanes == 64 + n % 48]).astype(np.float32), BF16)
    mask = jnp.asarray((np.arange(16)[:, None] == n // 48).astype(np.float32))
    out = pl.pallas_call(
        main_kernel,
        out_shape=jax.ShapeDtypeStruct((4616, LANES), F32),
        in_specs=[vmem] * 7,
        out_specs=vmem,
        scratch_shapes=[
            pltpu.VMEM((8, 32, LANES), BF16),
            pltpu.VMEM((2, 32, BLOCK), BF16),
            pltpu.VMEM((2, 32, BLOCK), BF16),
            pltpu.VMEM((2, 96, BLOCK), BF16),
            pltpu.VMEM((8, 8, C_ROWS, LANES), BF16),
            pltpu.VMEM((2048, BLOCK), F32),
            pltpu.VMEM((2048, BLOCK), BF16),
            pltpu.VMEM((2, 4, 96, 512), F32),
            pltpu.VMEM((4, 96, 512), F32),
            pltpu.VMEM((4, 96, 512), F32),
            pltpu.VMEM((3, 96, 512), F32),
            pltpu.VMEM((4, 192, 512), BF16),
            pltpu.VMEM((4, 2, 96, BLOCK), BF16),
            pltpu.VMEM((2, 96, BLOCK), BF16),
            pltpu.VMEM((2, 96, BLOCK), BF16),
            pltpu.VMEM((32, LANES), F32),
            pltpu.VMEM((8, LANES), F32),
            pltpu.VMEM((7, 8, LANES), F32),
            pltpu.VMEM((8, 8, LANES), F32),
            pltpu.VMEM((8, LANES), F32),
            dma((7,)), dma((7,)),
            dma((2,)), dma((2,)),
            dma((4,)), dma((4,)),
            dma((2, 2, 4)), dma((2, 2, 4)),
            dma((2, 2, 2, 4)), dma((2, 2, 2, 4)),
            dma((3,)), dma((3,)),
            dma((3,)), dma((3,)),
            dma((2, 3)), dma((2, 3)),
            dma, dma((7,)),
            dma((7,)), dma((7,)),
            dma((7,)), dma,
        ],
        compiler_params=pltpu.CompilerParams(
            collective_id=0, has_side_effects=True, vmem_limit_bytes=48 * 2**20
        ),
    )(msg, own, right, left, act_cot[0].T, pick, mask)
    return out.reshape(-1)[:SHARD]


def solution(mesh):
    placed = (P("dp", "fsdp", None), P("dp", None, "fsdp"), P("fsdp"), P())
    return jax.shard_map(body, mesh=mesh, in_specs=placed, out_specs=P("fsdp"), check_vma=False)
```

time: 1180 us -> 113 us (0.10)
  blocking collectives: 983 us -> 0 us
  Pallas kernels: 0 us -> 109 us
  waiting for transfers between devices: 74.1 us -> 0 us
  local copies, waits for them, and re-layouts: 64.2 us -> 3.2 us
  between operations: 16.8 us -> 0.08 us
  other arithmetic: 16.2 us -> 0 us
  matrix products: 12.3 us -> 0 us
    unnamed x1 -> x0, blocking collectives: 492 us -> none
    psum x1 -> x0, blocking collectives: 491 us -> none  [body(): gain_total = lax.psum(gain_part, 'fsdp')]
    pallas_call x0 -> x2, Pallas kernels: none -> 109 us  [the longest x1 104 us: body(): pl.pallas_call(main_kernel, out_shape=jax.ShapeDtypeStruct((4616, LANES),...]
    psum x1 -> x0, waiting for transfers between devices: 74 us -> none  [body(): return lax.psum(combined, 'dp')]
    concatenate x2 -> x0, local copies, waits for them, and re-layouts: 51.8 us -> none  [the longest x1 35.3 us: body(): jnp.concatenate([jnp.zeros((quarter,), jnp.bfloat16), old_slots, jnp.zero...]
    dot_general x3 -> x0, matrix products: 12.3 us -> none  [the longest x1 6.58 us: body(): lax.dot_general(pre_grad.astype(jnp.float32), normed, (((0,), (0,)), ((),...]
  transfers between devices with their start and end apart: 4 -> 0, of which waited for: 1 -> 0; matrix products, arithmetic and copies ran while one was open for 5% -> 0% of each run, Pallas kernels for 0% -> 0%
where the time goes in v1:
time: 113 us; the launch traced here: 112 us
  Pallas kernels  109 us (96%)
  local copies, waits for them, and re-layouts  3.2 us (3%)
    pallas_call x1, Pallas kernels, body(): pl.pallas_call(main_kernel, out_shape=jax.ShapeDtypeStruct((4616, LANES),...  104 us
    pallas_call x1, Pallas kernels, body(): pl.pallas_call(prepare_kernel, out_shape=[jax.ShapeDtypeStruct((8, 32, LA...  5.37 us

profile of v1, /device:TPU:1, one launch (start us, length us, event | category | flops | bytes accessed | tf_op | source)
XLA Modules:
  0.0 112.4 jit_solution(4991317991712666508)
XLA Ops:
  0.0 0.0 copy-start.4
  0.0 0.0 copy-start.2
  0.0 1.6 %pad_bitcast_fusion.slots_ref = bf16[6928,128]{1,0:T(8,128)(2,1)S(1)} fusion(bf16[884808]{0:T(1024)(128)(2,1)} %param.8), kind=kLoop, calls=%fused_computation | loop fusion | bytes 3543184 | tf_op jit(solution)/shard_map/reshape | solution.py:420
  1.6 0.0 copy-done.4
  1.6 0.0 copy-done.2
  1.6 0.0 copy-start
  1.7 0.0 copy-start.1
  1.7 0.0 copy-start.3
  1.7 5.4 %shard_map.64 = (bf16[8,32,128]{2,1,0:T(8,128)(2,1)S(1)}, bf16[2,96,768]{2,1,0:T(8,128)(2,1)S(1)}, bf16[2,32,768]{2,1,0:T(8,128)(2,1)S(1)}, bf16[2,32,768]{2,1,0:T(8,128)(2,1)S(1)}) custom-call(bf16[1,4,6144]{2,1,0:T(4,128)(2,1)S(1)} %copy-done.2, bf16[6928,128]{1,0:T(8,128)(2,1)S(1)} %pad_bitcast_fusion.slots_ref, s32[129]{0:T(256)S(1)} %copy-done.4), custom_call_target="tpu_custom_call" | custom-call | tf_op jit(solution)/shard_map/pallas_call | solution.py:421
  7.0 0.0 copy-done
  7.1 0.0 copy-done.1
  7.1 0.0 copy-done.3
  7.1 103.8 %shard_map.65 = f32[4616,128]{1,0:T(8,128)S(1)} custom-call(bf16[8,32,128]{2,1,0:T(8,128)(2,1)S(1)} %get-tuple-element.9.msg_ref, bf16[2,96,768]{2,1,0:T(8,128)(2,1)S(1)} %get-tuple-element.10.own_ref, bf16[2,32,768]{2,1,0:T(8,128)(2,1)S(1)} %get-tuple-element.11.right_ref, bf16[2,32,768]{2,1,0:T(8,128)(2,1)S(1)} %get-tuple-element.12.left_ref, ...), custom_call_target="tpu_custom_call" | custom-call | tf_op jit(solution)/shard_map/pallas_call | solution.py:443
  110.8 1.6 %copy.8 = f32[589872]{0:T(1024)} copy(f32[589872]{0:T(1024)S(1)} %bitcast.7) | data formatting | bytes 4718976
Async XLA Ops:
  0.0 1.6 %copy-start.4 = (s32[129]{0:T(256)S(1)}, s32[129]{0:T(256)}, u32[]{:S(2)}) copy-start(s32[129]{0:T(256)} %off_ref.1) | copy-start | bytes 1552
  0.0 1.6 %copy-start.2 = (bf16[1,4,6144]{2,1,0:T(4,128)(2,1)S(1)}, bf16[1,4,6144]{2,1,0:T(4,128)(2,1)}, u32[]{:S(2)}) copy-start(bf16[1,4,6144]{2,1,0:T(4,128)(2,1)} %tok_ref.1) | copy-start | bytes 147460
  1.6 5.4 %copy-start = (bf16[2,128,768]{2,1,0:T(8,128)(2,1)S(1)}, bf16[2,128,768]{2,1,0:T(8,128)(2,1)}, u32[]{:S(2)}) copy-start(bf16[2,128,768]{2,1,0:T(8,128)(2,1)} %constant.7.clone.pick_ref) | copy-start | bytes 1179652
  1.7 5.4 %copy-start.1 = (bf16[1,512,96]{1,2,0:T(8,128)(2,1)S(1)}, bf16[1,512,96]{1,2,0:T(8,128)(2,1)}, u32[]{:S(2)}) copy-start(bf16[1,512,96]{1,2,0:T(8,128)(2,1)} %param.7) | copy-start | bytes 294916
  1.7 5.4 %copy-start.3 = (f32[16,768]{1,0:T(8,128)S(1)}, f32[16,768]{1,0:T(8,128)}, u32[]{:S(2)}) copy-start(f32[16,768]{1,0:T(8,128)} %constant.8.clone.mask_ref) | copy-start | bytes 147460

commit v2 on v1

v2 whole, which is shorter than its diff:
```python
import jax
import jax.numpy as jnp
import numpy as np
from jax import lax
from jax.experimental import pallas as pl
from jax.experimental.pallas import tpu as pltpu
from jax.sharding import PartitionSpec as P

D = 6144
HID_DEV = 96
SHARD = 589872
EPSILON = 1e-06
LINES = 6928
FRONT = 2704
BACK = 384
BLOCK = 768
LANES = 128
A_ROWS = 112
B_ROWS = 96
F32 = jnp.float32
BF16 = jnp.bfloat16
AWAY = (0, 1, -1, 2, -2, 3, -3, 4)
SLOT = {d: n for n, d in enumerate(AWAY)}
SLOT[-4] = SLOT[4]
SETS = ((0, 128), (128, 256), (384, 128))


def chips_in_order():
    near = [(a, b) for b in range(4) for a in range(4)]
    mid = [(4 + e % 3, e // 3) for e in range(12)] + [(e % 7, 4 + e // 7) for e in range(20)]
    far = [(e, 7) for e in range(8)] + [(7 - e // 15, e - 8 - e // 15) for e in range(8, 16)]
    return near + mid + far


def lane_iota(rows):
    return lax.broadcasted_iota(jnp.int32, (rows, LANES), 1)


def three_terms(value):
    high = value.astype(BF16).astype(F32)
    rest = value - high
    mid = rest.astype(BF16).astype(F32)
    return high, mid, rest - mid


def gelu_slope(v):
    root = 0.7978845608028654
    t = jnp.tanh(root * (v + 0.044715 * (v * v * v)))
    return 0.5 * (1.0 + t) + 0.5 * v * (1.0 - t * t) * (root * (1.0 + 3 * 0.044715 * (v * v)))


def main_kernel(
    tok_ref, slots_ref, off_ref, cot_ref, away_ref, pick_ref, mask_ref, out_ref,
    wide, lines, packed, letters, mail, own, right_out, left_out, edge_right, edge_left,
    spill, weight, gath_a, gath_b, cot, norm, scaled,
    part_1, part_2, part_3, part_in_1, part_in_2, part_in_3,
    sums_1, sums_2, sums_3, sums_in_1, sums_in_2, sums_in_3, grads_1, grads_2, grads_3,
    acc, result, block_out, gain_own, gain_tiles, gain_rows, gain_mine, gain_z, gain_y, gain_out,
    mail_s, mail_r, edge_s, edge_r, core_s, core_r, one_s, one_r, two_s, two_r,
    half_s, half_r, sum_s, sum_r, pg_s, pg_r, pgc_s, pgc_r, res_s, res_r,
    gty_s, gty_r, gtz_s, gtz_r, gz_s, gz_r, gy_s, gy_r, gf_s, gf_r,
):
    part = (part_1, part_2, part_3)
    part_in = (part_in_1, part_in_2, part_in_3)
    sums = (sums_1, sums_2, sums_3)
    sums_in = (sums_in_1, sums_in_2, sums_in_3)
    grads = (grads_1, grads_2, grads_3)
    x = lax.axis_index("dp")
    f = lax.axis_index("fsdp")
    c = f % 2
    y = (f // 2) % 8
    z = f // 16
    g = 2 * x + c
    other = 1 - c
    su = 2 + 14 * c
    sv = 16 - 14 * c
    pu = y + c * (z - y)
    pv = z + c * (y - z)
    sends = []

    def at(xx, ff):
        return {"dp": xx, "fsdp": ff}

    def mate(gg):
        return at(gg // 2, f - c + gg % 2)

    def dev_u(d):
        return at(x, ((pu + d + 8) % 8) * su + pv * sv + c)

    def dev_v(d):
        return at(x, pu * su + ((pv + d + 8) % 8) * sv + c)

    def dev_y(d):
        return at(x, z * 16 + ((y + d) % 8) * 2 + c)

    def dev_z(d):
        return at(x, ((z + d) % 8) * 16 + y * 2 + c)

    def dev_x(d):
        return at((x + d + 4) % 4, f)

    core = at(x, f - c + other)
    right = at(x, (f + 1) % 128)
    left = at(x, (f + 127) % 128)

    def copy(src, dst, ssem, rsem, dev):
        return pltpu.make_async_remote_copy(
            src_ref=src, dst_ref=dst, send_sem=ssem, recv_sem=rsem,
            device_id=dev, device_id_type=pl.DeviceIdType.MESH,
        )

    def send(src, dst, ssem, rsem, dev):
        one = copy(src, dst, ssem, rsem, dev)
        one.start()
        sends.append(one)

    def arrive(dst, ssem, rsem):
        copy(dst, dst, ssem, rsem, core).wait_recv()

    barrier = pltpu.get_barrier_semaphore()
    peers = [mate((g + r) % 8) for r in range(1, 8)]
    peers += [dev_y(r) for r in range(1, 8)] + [dev_z(r) for r in range(1, 8)] + [right, left]
    for dev in peers:
        pl.semaphore_signal(barrier, inc=1, device_id=dev, device_id_type=pl.DeviceIdType.MESH)

    tok = tok_ref[0].astype(F32)
    mean = jnp.mean(tok, axis=-1, keepdims=True)
    centered = tok - mean
    variance = jnp.mean(centered * centered, axis=-1, keepdims=True)
    scale = lax.rsqrt(variance + EPSILON)
    lane4 = lane_iota(4)
    extra = jnp.zeros((4, LANES), F32)
    for n, term in enumerate(three_terms(mean) + three_terms(scale)):
        extra = jnp.where((lane4 == n) | (lane4 == n + 8), term, extra)
    for b in range(8):
        for k in range(6):
            col = (6 * b + k) * LANES
            packed[32 * b + 4 * k : 32 * b + 4 * k + 4, :] = tok[:, col : col + LANES]
        packed[32 * b + 24 : 32 * b + 28, :] = extra
        packed[32 * b + 28 : 32 * b + 32, :] = jnp.zeros((4, LANES), F32)
    for b in range(8):
        letters[b] = packed[32 * b : 32 * b + 32, :].astype(BF16)

    pl.semaphore_wait(barrier, len(peers))
    for r in range(1, 8):
        gg = (g + r) % 8
        send(letters.at[gg], mail.at[g], mail_s.at[r - 1], mail_r.at[r - 1], mate(gg))
    mail[pl.ds(g, 1)] = letters[pl.ds(g, 1)]

    start = off_ref[f]
    length = off_ref[f + 1] - start
    shift_own = f * SHARD - start
    shift_right = shift_own + SHARD
    shift_left = shift_own - SHARD

    def widen(i, carry):
        rows = pl.ds(pl.multiple_of(i * 16, 16), 16)
        wide[pl.ds(pl.multiple_of(FRONT + i * 16, 16), 16), :] = slots_ref[rows, :].astype(F32)
        return carry

    lax.fori_loop(0, LINES // 16, widen, 0, unroll=8)

    def extract(first, shift, rows):
        turn = shift & (LANES - 1)
        row = FRONT + first + lax.shift_right_arithmetic(shift, 7)
        row = jnp.clip(row, 0, FRONT + LINES + BACK - rows - 1)
        here = wide[pl.ds(row, rows), :]
        after = wide[pl.ds(row + 1, rows), :]
        back = (LANES - turn) & (LANES - 1)
        lane = lane_iota(rows)
        line = lax.broadcasted_iota(jnp.int32, (rows, LANES), 0)
        moved = jnp.where(lane < LANES - turn, pltpu.roll(here, back, 1), pltpu.roll(after, back, 1))
        slot = (first + line) * LANES + lane + shift
        return jnp.where((slot >= 0) & (slot < length), moved, 0.0)

    def piece(piece_ref, first_row, rows, shift, top=None):
        def one(h, carry):
            got = extract((first_row + h) * 48 + 12 * x, shift, 16)
            lines[pl.ds(pl.multiple_of(h * 16, 16), 16), :] = got
            return carry

        lax.fori_loop(0, rows, one, 0, unroll=4)
        if top is not None:
            lines[0:1, :] = top
        for k in range(12):
            col = lines[pl.ds(k, rows, stride=16), :]
            piece_ref[k // 6, :, (k % 6) * LANES : (k % 6 + 1) * LANES] = col.astype(BF16)

    piece(left_out, 64, 32, shift_left, extract(0, shift_left + HID_DEV * D - 16, 8)[0:1])
    send(left_out, edge_left, edge_s.at[1], edge_r.at[1], left)
    piece(right_out, 0, 32, shift_right)
    send(right_out, edge_right, edge_s.at[0], edge_r.at[0], right)
    gain_own[...] = extract(0, shift_own + HID_DEV * D - 16, 8)

    for r in range(1, 8):
        arrive(mail.at[(g - r + 8) % 8], mail_s.at[r - 1], mail_r.at[r - 1])

    posts = mail[...].reshape(256, LANES)
    out_row = lax.broadcasted_iota(jnp.int32, (A_ROWS + B_ROWS, 256), 0)
    in_row = lax.broadcasted_iota(jnp.int32, (A_ROWS + B_ROWS, 256), 1)
    token = out_row & 31
    want = 32 * (token >> 2) + 4 * (out_row >> 5) + (token & 3)
    chunk = jnp.dot((want == in_row).astype(BF16), posts, preferred_element_type=F32)
    out_row = lax.broadcasted_iota(jnp.int32, (16, 256), 0) + 16
    in_row = lax.broadcasted_iota(jnp.int32, (16, 256), 1)
    want = 32 * (out_row >> 2) + 24 + (out_row & 3)
    late = jnp.dot((want == in_row).astype(BF16), posts, preferred_element_type=F32)
    lane = lane_iota(16)
    stats = jnp.where((lane >= 8) & (lane < 16), late, chunk[192:208])
    gath_a[0, 0] = chunk[0:A_ROWS].astype(BF16)
    gath_b[0, 0, 0:80, :] = chunk[A_ROWS:192].astype(BF16)
    gath_b[0, 0, 80:96, :] = stats.astype(BF16)

    for d in (1, -1, 2, -2, 3, -3, 4):
        n = SLOT[-d]
        send(gath_a.at[0, 0], gath_a.at[n, 0], one_s.at[0, n - 1], one_r.at[0, n - 1], dev_u(d))
        send(gath_b.at[0, 0], gath_b.at[0, n], one_s.at[1, n - 1], one_r.at[1, n - 1], dev_v(d))

    piece(own, 0, 96, shift_own)

    def unit_a(h, n):
        return gath_a.at[4 * h : 4 * h + 4, n]

    def unit_b(h, n):
        return gath_b.at[n, 4 * h : 4 * h + 4]

    streams = ((unit_a, dev_v, 1), (unit_a, dev_v, -1), (unit_b, dev_u, 1), (unit_b, dev_u, -1))

    def lands(s, h):
        for n, (unit, dev, d) in enumerate(streams):
            if s < 4 or (h == 0) == (d == 1):
                arrive(unit(h, SLOT[-d * s]), two_s.at[n, h, s - 1], two_r.at[n, h, s - 1])

    def onward(s, h):
        for n, (unit, dev, d) in enumerate(streams):
            if s < 4 or (h == 0) == (d == 1):
                send(
                    unit(h, SLOT[-d * (s - 1)]), unit(h, SLOT[-d * s]),
                    two_s.at[n, h, s - 1], two_r.at[n, h, s - 1], dev(d),
                )

    for n in (1, 2, 3):
        arrive(gath_a.at[n, 0], one_s.at[0, n - 1], one_r.at[0, n - 1])
        arrive(gath_b.at[0, n], one_s.at[1, n - 1], one_r.at[1, n - 1])
    onward(1, 0)
    for n in (4, 5, 6, 7):
        arrive(gath_a.at[n, 0], one_s.at[0, n - 1], one_r.at[0, n - 1])
        arrive(gath_b.at[0, n], one_s.at[1, n - 1], one_r.at[1, n - 1])
    onward(1, 1)

    arrive(edge_right, edge_s.at[0], edge_r.at[0])
    arrive(edge_left, edge_s.at[1], edge_r.at[1])
    row32 = lax.broadcasted_iota(jnp.int32, (32, BLOCK), 0)
    for half in range(2):
        spill[half, 0:32, :] = own[half, 0:32, :] + edge_right[half]
        spill[half, 32:64, :] = own[half, 32:64, :]
        low = jnp.where(row32 >= 8, edge_left[half].astype(F32), 0.0)
        spill[half, 64:96, :] = (own[half, 64:96, :].astype(F32) + low).astype(BF16)
        spill[half, 96:112, :] = jnp.zeros((16, BLOCK), BF16)
        first16 = edge_left[0, 0:16, 0:LANES].astype(F32)[0:8] + gain_own[...]
        lane8 = lane_iota(8)
        first16 = jnp.where((lane8 >= 16) & (lane8 < 64), first16, 0.0)
        first16 = jnp.concatenate([first16, jnp.zeros((8, LANES), F32)], axis=0)
        spill[half, 96:112, 0:LANES] = first16.astype(BF16)
    send(spill.at[other], weight.at[c], core_s.at[0], core_r.at[0], core)
    weight[pl.ds(c, 1)] = spill[pl.ds(c, 1)]

    lands(1, 0)
    onward(2, 0)

    arrive(weight.at[other], core_s.at[0], core_r.at[0])
    apart = (z - g + 8) % 8
    outs = [
        copy(gain_tiles.at[y], gain_tiles.at[y], gty_s.at[r - 1], gty_r.at[r - 1], dev_y(r)) for r in range(1, 8)
    ]

    @pl.when(apart == 0)
    def _():
        rows = jnp.concatenate(
            [weight[half, 96:112, 0:LANES].astype(F32)[0:1] for half in range(2)] + [jnp.zeros((6, LANES), F32)], axis=0
        )
        gain_tiles[pl.ds(y, 1)] = rows[None]
        for one in outs:
            one.start()

    lands(1, 1)
    onward(2, 1)

    t = lax.broadcasted_iota(jnp.int32, (1, 512), 1)
    home = (((z + 8 + away_ref[1:2, :]) & 7) * 8 + ((y + 8 + away_ref[0:1, :]) & 7)) * 8 + (t & 7)
    nat = lax.broadcasted_iota(jnp.int32, (512, 512), 0)
    cot[...] = jnp.dot(cot_ref[...], (nat == home).astype(BF16), preferred_element_type=F32)

    outs_z = [copy(gain_tiles, gain_tiles, gtz_s.at[r - 1], gtz_r, dev_z(r)) for r in range(1, 8)]

    @pl.when(apart == 0)
    def _():
        for r in range(1, 8):
            arrive(gain_tiles.at[(y - r + 8) % 8], gty_s.at[r - 1], gty_r.at[r - 1])
        for one in outs:
            one.wait_send()
        for one in outs_z:
            one.start()
        for one in outs_z:
            one.wait_send()

    lands(2, 0)
    onward(3, 0)

    @pl.when(apart != 0)
    def _():
        arrive(gain_tiles, gtz_s.at[0], gtz_r)

    for yy in range(8):
        gain_rows[2 * yy : 2 * yy + 2, :] = gain_tiles[yy, 0:2, :]
    spread = jnp.dot(gain_rows[...].astype(BF16), pick_ref[...], preferred_element_type=F32)
    gain = jnp.sum(spread * mask_ref[...], axis=0, keepdims=True)

    def normalize(first, places):
        data = []
        for a, b in places:
            uu, vv = a + c * (b - a), b + c * (a - b)
            rows = gath_b[uu, vv, 80:96, :].astype(F32)
            cols = []
            for base in (0, 3):
                early = (rows[:, base : base + 1] + rows[:, base + 1 : base + 2]) + rows[:, base + 2 : base + 3]
                late = (rows[:, base + 8 : base + 9] + rows[:, base + 9 : base + 10]) + rows[:, base + 10 : base + 11]
                cols.append((early[0:8], early[8:16], late[0:8], late[8:16]))
            data.append((uu, vv, cols))
        for k in range(6):
            gain_k = gain[:, k * LANES : (k + 1) * LANES]
            tiles = []
            for uu, vv, _ in data:
                if k < 3:
                    tile = gath_a[uu, vv, 32 * k : 32 * k + 32, :].astype(F32)
                elif k == 3:
                    tile = jnp.concatenate(
                        [gath_a[uu, vv, 96:112, :].astype(F32), gath_b[uu, vv, 0:16, :].astype(F32)], axis=0
                    )
                else:
                    tile = gath_b[uu, vv, 32 * k - 112 : 32 * k - 80, :].astype(F32)
                tiles.append(tile)
            for xx in range(4):
                both = jnp.concatenate(
                    [
                        (tiles[side][8 * xx : 8 * xx + 8] - data[side][2][0][xx]) * data[side][2][1][xx]
                        for side in range(2)
                    ],
                    axis=0,
                )
                rows = pl.ds(pl.multiple_of(512 * xx + 8 * first, 16), 16)
                norm[rows, k * LANES : (k + 1) * LANES] = both
                scaled[rows, k * LANES : (k + 1) * LANES] = (both * gain_k).astype(BF16)

    def pairs(low, high, first, place):
        def one(p, carry):
            normalize(first + 2 * p, (place(2 * p), place(2 * p + 1)))
            return carry

        lax.fori_loop(low, high, one, 0)

    block = weight[:, 0:96, :].reshape(192, BLOCK)

    def pre_act(n):
        low, size = SETS[n]
        for xx in range(4):
            got = lax.dot_general(
                block, scaled[512 * xx + low : 512 * xx + low + size, :], (((1,), (1,)), ((), ())),
                preferred_element_type=F32,
            )
            part[n][0, xx] = got[0:96]
            part[n][1, xx] = got[96:192]
        send(part[n].at[other], part_in[n], half_s.at[n], half_r.at[n], core)

    def sum_x(n):
        arrive(part_in[n], half_s.at[n], half_r.at[n])
        sums[n][...] = part[n][pl.ds(c, 1)][0] + part_in[n][...]
        for r in range(1, 4):
            send(sums[n].at[(x + r) % 4], sums_in[n].at[r - 1], sum_s.at[n, r - 1], sum_r.at[n, r - 1], dev_x(r))

    mine = pl.ds(pl.multiple_of(96 * c, 32), 96)
    theirs = pl.ds(pl.multiple_of(96 * other, 32), 96)

    def slope(n):
        low, size = SETS[n]
        for r in range(1, 4):
            arrive(sums_in[n].at[r - 1], sum_s.at[n, r - 1], sum_r.at[n, r - 1])
        total = (sums[n][pl.ds(x, 1)][0] + sums_in[n][0]) + (sums_in[n][1] + sums_in[n][2])
        grads[n][pl.ds(x, 1), mine, :] = (cot[:, low : low + size] * gelu_slope(total)).astype(BF16)[None]
        for r in range(1, 4):
            send(grads[n].at[x, mine], grads[n].at[x, mine], pg_s.at[n, r - 1], pg_r.at[n, r - 1], dev_x(r))

    def share(n):
        for r in range(1, 4):
            arrive(grads[n].at[(x - r + 4) % 4, mine], pg_s.at[n, r - 1], pg_r.at[n, r - 1])
        send(grads[n].at[:, mine], grads[n].at[:, mine], pgc_s.at[n], pgc_r.at[n], core)

    def shared(n):
        arrive(grads[n].at[:, theirs], pgc_s.at[n], pgc_r.at[n])

    def gradient(n):
        low, size = SETS[n]
        total = jnp.zeros((192, BLOCK), F32)
        for xx in range(4):
            rows = scaled[512 * xx + low : 512 * xx + low + size, :]
            total += jnp.dot(grads[n][xx], rows, preferred_element_type=F32)
        return total

    def gain_part(n):
        low, size = SETS[n]
        total = jnp.zeros((1, BLOCK), F32)
        for xx in range(4):
            back = lax.dot_general(grads[n][xx], block, (((0,), (0,)), ((), ())), preferred_element_type=F32)
            rows = norm[512 * xx + low : 512 * xx + low + size, :]
            total += jnp.sum(back * rows, axis=0, keepdims=True)
        return total

    pairs(0, 8, 0, lambda e: (e % 4, e // 4))
    pre_act(0)

    lands(2, 1)
    onward(3, 1)
    lands(3, 0)
    onward(4, 0)
    sum_x(0)
    lands(3, 1)
    onward(4, 1)

    pairs(0, 6, 16, lambda e: (4 + e % 3, e // 3))
    pairs(0, 10, 28, lambda e: (e % 7, 4 + e // 7))
    pre_act(1)
    slope(0)

    lands(4, 0)
    lands(4, 1)
    pairs(0, 4, 48, lambda e: (e, 7))
    pairs(4, 8, 48, lambda e: (7 - e // 15, e - 8 - e // 15))
    sum_x(1)
    pre_act(2)
    share(0)
    sum_x(2)
    shared(0)
    acc[...] = gradient(0)
    slope(1)
    gain_sum = gain_part(0)
    slope(2)
    share(1)
    share(2)
    shared(1)
    acc[...] += gradient(1)
    gain_sum += gain_part(1)
    shared(2)
    rounded = (acc[...] + gradient(2)).astype(BF16)

    block_out[0] = rounded[0:96]
    block_out[1] = rounded[96:192]
    send(block_out.at[other], result.at[x, c], core_s.at[1], core_r.at[1], core)
    result[pl.ds(x, 1), pl.ds(c, 1)] = block_out[pl.ds(c, 1)][None]
    for m, d in enumerate((1, -1)):
        send(result.at[x, c], result.at[x, c], res_s.at[m, 0], res_r.at[m, 0], dev_x(d))
    gain_sum += gain_part(2)
    for k in range(6):
        gain_mine[k : k + 1, :] = gain_sum[:, k * LANES : (k + 1) * LANES]
    gain_mine[6:8, :] = jnp.zeros((2, LANES), F32)
    arrive(result.at[x, other], core_s.at[1], core_r.at[1])
    for m, d in enumerate((1, -1)):
        send(result.at[x, other], result.at[x, other], res_s.at[m, 1], res_r.at[m, 1], dev_x(d))

    to_z = copy(gain_mine, gain_z.at[(apart + 7) % 8], gz_s, gz_r.at[(apart + 7) % 8], at(x, g * 16 + y * 2 + c))

    @pl.when(apart != 0)
    def _():
        to_z.start()

    def spell(xx, half):
        for k in range(6):
            col = result[xx, half, :, k * LANES : (k + 1) * LANES].astype(F32)
            out_ref[pl.ds(12 * xx + 6 * half + k, 96, stride=48), :] = col

    for half in range(2):
        spell(x, half)

    outs_y = [copy(gain_y.at[7], gain_y.at[r - 1], gy_s.at[r - 1], gy_r.at[r - 1], dev_y(r)) for r in range(1, 8)]

    @pl.when(apart == 0)
    def _():
        sum_z = gain_mine[...]
        for r in range(7):
            arrive(gain_z.at[r], gz_s, gz_r.at[r])
            sum_z += gain_z[r]
        gain_y[7] = sum_z
        for one in outs_y:
            one.start()

    arrive(result.at[(x + 3) % 4, c], res_s.at[0, 0], res_r.at[0, 0])
    arrive(result.at[(x + 1) % 4, c], res_s.at[1, 0], res_r.at[1, 0])
    arrive(result.at[(x + 3) % 4, other], res_s.at[0, 1], res_r.at[0, 1])
    send(result.at[(x + 3) % 4, 0], result.at[(x + 3) % 4, 0], res_s.at[0, 2], res_r.at[0, 2], dev_x(1))
    arrive(result.at[(x + 1) % 4, other], res_s.at[1, 1], res_r.at[1, 1])
    send(result.at[(x + 1) % 4, 1], result.at[(x + 1) % 4, 1], res_s.at[1, 2], res_r.at[1, 2], dev_x(-1))

    outs_f = [copy(gain_out, gain_out, gf_s.at[r - 1], gf_r, mate((g + r) % 8)) for r in range(1, 8)]

    @pl.when(apart == 0)
    def _():
        sum_y = gain_y[7]
        for r in range(7):
            arrive(gain_y.at[r], gy_s.at[r], gy_r.at[r])
            sum_y += gain_y[r]
        gain_out[...] = sum_y
        for one in outs_f:
            one.start()

    for half in range(2):
        spell((x + 3) % 4, half)
        spell((x + 1) % 4, half)

    @pl.when(apart != 0)
    def _():
        arrive(gain_out, gf_s.at[0], gf_r)
        to_z.wait_send()

    @pl.when(apart == 0)
    def _():
        for one in outs_y:
            one.wait_send()
        for one in outs_f:
            one.wait_send()

    first = 48 * (2 * y + c)
    turn = first % LANES
    line = first // LANES
    here = jnp.broadcast_to(gain_out[pl.ds(line, 1), :], (8, LANES))
    after = jnp.broadcast_to(gain_out[pl.ds(line + 1, 1), :], (8, LANES))
    back = (LANES - turn) % LANES
    moved = jnp.where(lane_iota(8) < LANES - turn, pltpu.roll(here, back, 1), pltpu.roll(after, back, 1))
    out_ref[4608:4616, :] = moved

    arrive(result.at[(x + 2) % 4, 0], res_s.at[0, 2], res_r.at[0, 2])
    spell((x + 2) % 4, 0)
    arrive(result.at[(x + 2) % 4, 1], res_s.at[1, 2], res_r.at[1, 2])
    spell((x + 2) % 4, 1)
    for one in sends:
        one.wait_send()


def body(tokens, act_cot, old_slots, offsets):
    vmem = pl.BlockSpec(memory_space=pltpu.VMEM)
    smem = pl.BlockSpec(memory_space=pltpu.SMEM)
    dma = pltpu.SemaphoreType.DMA
    slots = jnp.pad(old_slots, (0, LINES * LANES - old_slots.shape[0])).reshape(LINES, LANES)
    chips = chips_in_order()
    away = np.array([[AWAY[chip[axis]] for chip in chips for _ in range(8)] for axis in range(2)], np.int32)
    n = np.arange(BLOCK)
    lanes = np.arange(LANES)[:, None]
    pick = jnp.asarray((lanes == 16 + n % 48).astype(np.float32), BF16)
    mask = jnp.asarray((np.arange(16)[:, None] == n // 48).astype(np.float32))
    out = pl.pallas_call(
        main_kernel,
        out_shape=jax.ShapeDtypeStruct((4616, LANES), F32),
        in_specs=[vmem, vmem, smem, vmem, vmem, vmem, vmem],
        out_specs=vmem,
        scratch_shapes=[
            pltpu.VMEM((FRONT + LINES + BACK, LANES), F32),
            pltpu.VMEM((96 * 16, LANES), F32),
            pltpu.VMEM((256, LANES), F32),
            pltpu.VMEM((8, 32, LANES), BF16),
            pltpu.VMEM((8, 32, LANES), BF16),
            pltpu.VMEM((2, 96, BLOCK), BF16),
            pltpu.VMEM((2, 32, BLOCK), BF16),
            pltpu.VMEM((2, 32, BLOCK), BF16),
            pltpu.VMEM((2, 32, BLOCK), BF16),
            pltpu.VMEM((2, 32, BLOCK), BF16),
            pltpu.VMEM((2, 112, BLOCK), BF16),
            pltpu.VMEM((2, 112, BLOCK), BF16),
            pltpu.VMEM((8, 8, A_ROWS, LANES), BF16),
            pltpu.VMEM((8, 8, B_ROWS, LANES), BF16),
            pltpu.VMEM((96, 512), F32),
            pltpu.VMEM((2048, BLOCK), F32),
            pltpu.VMEM((2048, BLOCK), BF16),
            *[pltpu.VMEM((2, 4, 96, size), F32) for _, size in SETS],
            *[pltpu.VMEM((4, 96, size), F32) for _, size in SETS],
            *[pltpu.VMEM((4, 96, size), F32) for _, size in SETS],
            *[pltpu.VMEM((3, 96, size), F32) for _, size in SETS],
            *[pltpu.VMEM((4, 192, size), BF16) for _, size in SETS],
            pltpu.VMEM((192, BLOCK), F32),
            pltpu.VMEM((4, 2, 96, BLOCK), BF16),
            pltpu.VMEM((2, 96, BLOCK), BF16),
            pltpu.VMEM((8, LANES), F32),
            pltpu.VMEM((8, 8, LANES), F32),
            pltpu.VMEM((16, LANES), F32),
            pltpu.VMEM((8, LANES), F32),
            pltpu.VMEM((8, 8, LANES), F32),
            pltpu.VMEM((8, 8, LANES), F32),
            pltpu.VMEM((8, LANES), F32),
            dma((7,)), dma((7,)),
            dma((2,)), dma((2,)),
            dma((2,)), dma((2,)),
            dma((2, 7)), dma((2, 7)),
            dma((4, 2, 4)), dma((4, 2, 4)),
            dma((3,)), dma((3,)),
            dma((3, 3)), dma((3, 3)),
            dma((3, 3)), dma((3, 3)),
            dma((3,)), dma((3,)),
            dma((2, 3)), dma((2, 3)),
            dma((7,)), dma((7,)),
            dma((7,)), dma,
            dma, dma((8,)),
            dma((7,)), dma((7,)),
            dma((7,)), dma,
        ],
        compiler_params=pltpu.CompilerParams(
            collective_id=0, has_side_effects=True, vmem_limit_bytes=56 * 2**20
        ),
    )(tokens, slots, offsets, act_cot[0].T, jnp.asarray(away), pick, mask)
    return out.reshape(-1)[:SHARD]


def solution(mesh):
    placed = (P("dp", "fsdp", None), P("dp", None, "fsdp"), P("fsdp"), P())
    return jax.shard_map(body, mesh=mesh, in_specs=placed, out_specs=P("fsdp"), check_vma=False)
```

time: 113 us -> 95.4 us (0.84)
  Pallas kernels: 109 us -> 89.2 us
  local copies, waits for them, and re-layouts: 3.2 us -> 6.03 us
    pallas_call x1, Pallas kernels: 104 us -> 89.2 us  [body(): pl.pallas_call(main_kernel, out_shape=jax.ShapeDtypeStruct((4616, LANES),...]
    pallas_call x1 -> x0, Pallas kernels: 5.37 us -> none  [body(): pl.pallas_call(prepare_kernel, out_shape=[jax.ShapeDtypeStruct((8, 32, LA...]
    unnamed x11 -> x1, local copies, waits for them, and re-layouts: 1.59 us -> 3.23 us
    reshape x1, local copies, waits for them, and re-layouts: 1.61 us -> 2.8 us  [body(): jnp.pad(old_slots, (0, LINES * LANES - old_slots.shape[0]))]
where the time goes in v2:
time: 95.4 us; the launch traced here: 95.2 us
  Pallas kernels  89.2 us (94%)
  local copies, waits for them, and re-layouts  6.03 us (6%)
    pallas_call x1, Pallas kernels, body(): pl.pallas_call(main_kernel, out_shape=jax.ShapeDtypeStruct((4616, LANES),...  89.2 us
    unnamed x1, local copies, waits for them, and re-layouts  3.23 us
    reshape x1, local copies, waits for them, and re-layouts, body(): jnp.pad(old_slots, (0, LINES * LANES - old_slots.shape[0]))  2.8 us

profile of v2, /device:TPU:1, one launch (start us, length us, event | category | flops | bytes accessed | tf_op | source)
XLA Modules:
  0.0 95.2 jit_solution(15313715639499869599)
XLA Ops:
  0.0 2.8 %pad_bitcast_fusion.slots_ref = bf16[6928,128]{1,0:T(8,128)(2,1)} fusion(bf16[884808]{0:T(1024)(128)(2,1)} %param.9), kind=kLoop, calls=%fused_computation | loop fusion | bytes 3543184 | tf_op jit(solution)/shard_map/reshape | solution.py:551
  2.8 89.2 %shard_map.73 = f32[4616,128]{1,0:T(8,128)} custom-call(bf16[1,4,6144]{2,1,0:T(4,128)(2,1)} %tok_ref.1, bf16[6928,128]{1,0:T(8,128)(2,1)} %pad_bitcast_fusion.slots_ref, s32[129]{0:T(256)} %off_ref.1, bf16[96,512]{1,0:T(8,128)(2,1)} %bitcast.8, s32[2,512]{1,0:T(2,128)} %constant.11.clone.away_ref, bf16[128,768]{1,0:T(8,128)(2,1)} %constant.9.clone.pick_ref, ...), custom_call_target="tpu_custom_call" | custom-call | tf_op jit(solution)/shard_map/pallas_call | solution.py:558
  92.0 3.2 %copy.9 = f32[589872]{0:T(1024)} copy(f32[589872]{0:T(1024)} %bitcast.7) | data formatting | bytes 4718976

commit v3 on v2

--- a/solution.py
+++ b/solution.py
@@ -52,7 +52,7 @@
 def main_kernel(
     tok_ref, slots_ref, off_ref, cot_ref, away_ref, pick_ref, mask_ref, out_ref,
     wide, lines, packed, letters, mail, own, right_out, left_out, edge_right, edge_left,
-    spill, weight, gath_a, gath_b, cot, norm, scaled,
+    spill, weight, gain_pair, gath_a, gath_b, cot, norm, scaled,
     part_1, part_2, part_3, part_in_1, part_in_2, part_in_3,
     sums_1, sums_2, sums_3, sums_in_1, sums_in_2, sums_in_3, grads_1, grads_2, grads_3,
     acc, result, block_out, gain_own, gain_tiles, gain_rows, gain_mine, gain_z, gain_y, gain_out,
@@ -173,22 +173,25 @@
         slot = (first + line) * LANES + lane + shift
         return jnp.where((slot >= 0) & (slot < length), moved, 0.0)
 
-    def piece(piece_ref, first_row, rows, shift, top=None):
+    def move(first_row, low, high, shift):
         def one(h, carry):
             got = extract((first_row + h) * 48 + 12 * x, shift, 16)
             lines[pl.ds(pl.multiple_of(h * 16, 16), 16), :] = got
             return carry
 
-        lax.fori_loop(0, rows, one, 0, unroll=4)
-        if top is not None:
-            lines[0:1, :] = top
+        lax.fori_loop(low, high, one, 0, unroll=4)
+
+    def keep(piece_ref, rows):
         for k in range(12):
             col = lines[pl.ds(k, rows, stride=16), :]
             piece_ref[k // 6, :, (k % 6) * LANES : (k % 6 + 1) * LANES] = col.astype(BF16)
 
-    piece(left_out, 64, 32, shift_left, extract(0, shift_left + HID_DEV * D - 16, 8)[0:1])
+    move(64, 0, 32, shift_left)
+    lines[0:1, :] = extract(0, shift_left + HID_DEV * D - 16, 8)[0:1]
+    keep(left_out, 32)
     send(left_out, edge_left, edge_s.at[1], edge_r.at[1], left)
-    piece(right_out, 0, 32, shift_right)
+    move(0, 0, 32, shift_right)
+    keep(right_out, 32)
     send(right_out, edge_right, edge_s.at[0], edge_r.at[0], right)
     gain_own[...] = extract(0, shift_own + HID_DEV * D - 16, 8)
 
@@ -216,81 +219,89 @@
         send(gath_a.at[0, 0], gath_a.at[n, 0], one_s.at[0, n - 1], one_r.at[0, n - 1], dev_u(d))
         send(gath_b.at[0, 0], gath_b.at[0, n], one_s.at[1, n - 1], one_r.at[1, n - 1], dev_v(d))
 
-    piece(own, 0, 96, shift_own)
+    move(0, 0, 32, shift_own)
+    arrive(edge_left, edge_s.at[1], edge_r.at[1])
+    lane8 = lane_iota(8)
+    gain_row = edge_left[0, 0:16, 0:LANES].astype(F32)[0:8] + gain_own[...]
+    gain_pair[pl.ds(c, 1)] = jnp.where((lane8 >= 16) & (lane8 < 64), gain_row, 0.0)[None]
+    send(gain_pair.at[c], gain_pair.at[c], core_s.at[2], core_r.at[2], core)
+    move(0, 32, 64, shift_own)
+    arrive(gain_pair.at[other], core_s.at[2], core_r.at[2])
+    apart = (z - g + 8) % 8
+    outs = [
+        copy(gain_tiles.at[y], gain_tiles.at[y], gty_s.at[r - 1], gty_r.at[r - 1], dev_y(r)) for r in range(1, 8)
+    ]
+
+    @pl.when(apart == 0)
+    def _():
+        rows = jnp.concatenate([gain_pair[0, 0:1], gain_pair[1, 0:1], jnp.zeros((6, LANES), F32)], axis=0)
+        gain_tiles[pl.ds(y, 1)] = rows[None]
+        for one in outs:
+            one.start()
 
     def unit_a(h, n):
-        return gath_a.at[4 * h : 4 * h + 4, n]
+        return gath_a.at[2 * h : 2 * h + 2, n]
 
     def unit_b(h, n):
-        return gath_b.at[n, 4 * h : 4 * h + 4]
+        return gath_b.at[n, 2 * h : 2 * h + 2]
 
     streams = ((unit_a, dev_v, 1), (unit_a, dev_v, -1), (unit_b, dev_u, 1), (unit_b, dev_u, -1))
 
     def lands(s, h):
         for n, (unit, dev, d) in enumerate(streams):
-            if s < 4 or (h == 0) == (d == 1):
+            if s < 4 or (h < 2) == (d == 1):
                 arrive(unit(h, SLOT[-d * s]), two_s.at[n, h, s - 1], two_r.at[n, h, s - 1])
 
     def onward(s, h):
+        if s > 1:
+            lands(s - 1, h)
         for n, (unit, dev, d) in enumerate(streams):
-            if s < 4 or (h == 0) == (d == 1):
+            if s < 4 or (h < 2) == (d == 1):
                 send(
                     unit(h, SLOT[-d * (s - 1)]), unit(h, SLOT[-d * s]),
                     two_s.at[n, h, s - 1], two_r.at[n, h, s - 1], dev(d),
                 )
 
-    for n in (1, 2, 3):
+    def first_axis(n):
         arrive(gath_a.at[n, 0], one_s.at[0, n - 1], one_r.at[0, n - 1])
         arrive(gath_b.at[0, n], one_s.at[1, n - 1], one_r.at[1, n - 1])
+
+    first_axis(1)
     onward(1, 0)
-    for n in (4, 5, 6, 7):
-        arrive(gath_a.at[n, 0], one_s.at[0, n - 1], one_r.at[0, n - 1])
-        arrive(gath_b.at[0, n], one_s.at[1, n - 1], one_r.at[1, n - 1])
+    first_axis(2)
+    first_axis(3)
     onward(1, 1)
-
+    move(0, 64, 96, shift_own)
+    first_axis(4)
+    first_axis(5)
+    onward(1, 2)
+    first_axis(6)
+    first_axis(7)
+    onward(1, 3)
+
+    keep(own, 96)
     arrive(edge_right, edge_s.at[0], edge_r.at[0])
-    arrive(edge_left, edge_s.at[1], edge_r.at[1])
     row32 = lax.broadcasted_iota(jnp.int32, (32, BLOCK), 0)
     for half in range(2):
         spill[half, 0:32, :] = own[half, 0:32, :] + edge_right[half]
         spill[half, 32:64, :] = own[half, 32:64, :]
         low = jnp.where(row32 >= 8, edge_left[half].astype(F32), 0.0)
         spill[half, 64:96, :] = (own[half, 64:96, :].astype(F32) + low).astype(BF16)
-        spill[half, 96:112, :] = jnp.zeros((16, BLOCK), BF16)
-        first16 = edge_left[0, 0:16, 0:LANES].astype(F32)[0:8] + gain_own[...]
-        lane8 = lane_iota(8)
-        first16 = jnp.where((lane8 >= 16) & (lane8 < 64), first16, 0.0)
-        first16 = jnp.concatenate([first16, jnp.zeros((8, LANES), F32)], axis=0)
-        spill[half, 96:112, 0:LANES] = first16.astype(BF16)
     send(spill.at[other], weight.at[c], core_s.at[0], core_r.at[0], core)
     weight[pl.ds(c, 1)] = spill[pl.ds(c, 1)]
-
-    lands(1, 0)
     onward(2, 0)
 
-    arrive(weight.at[other], core_s.at[0], core_r.at[0])
-    apart = (z - g + 8) % 8
-    outs = [
-        copy(gain_tiles.at[y], gain_tiles.at[y], gty_s.at[r - 1], gty_r.at[r - 1], dev_y(r)) for r in range(1, 8)
-    ]
-
-    @pl.when(apart == 0)
-    def _():
-        rows = jnp.concatenate(
-            [weight[half, 96:112, 0:LANES].astype(F32)[0:1] for half in range(2)] + [jnp.zeros((6, LANES), F32)], axis=0
-        )
-        gain_tiles[pl.ds(y, 1)] = rows[None]
-        for one in outs:
-            one.start()
-
-    lands(1, 1)
+    def reorder(low):
+        t = lax.broadcasted_iota(jnp.int32, (1, 256), 1)
+        away_y, away_z = away_ref[0:1, low : low + 256], away_ref[1:2, low : low + 256]
+        home = (((z + 8 + away_z) & 7) * 8 + ((y + 8 + away_y) & 7)) * 8 + (t & 7)
+        nat = lax.broadcasted_iota(jnp.int32, (512, 256), 0)
+        cot[:, low : low + 256] = jnp.dot(cot_ref[...], (nat == home).astype(BF16), preferred_element_type=F32)
+
+    reorder(0)
     onward(2, 1)
-
-    t = lax.broadcasted_iota(jnp.int32, (1, 512), 1)
-    home = (((z + 8 + away_ref[1:2, :]) & 7) * 8 + ((y + 8 + away_ref[0:1, :]) & 7)) * 8 + (t & 7)
-    nat = lax.broadcasted_iota(jnp.int32, (512, 512), 0)
-    cot[...] = jnp.dot(cot_ref[...], (nat == home).astype(BF16), preferred_element_type=F32)
-
+    reorder(256)
+    onward(2, 2)
     outs_z = [copy(gain_tiles, gain_tiles, gtz_s.at[r - 1], gtz_r, dev_z(r)) for r in range(1, 8)]
 
     @pl.when(apart == 0)
@@ -301,15 +312,20 @@
             one.wait_send()
         for one in outs_z:
             one.start()
+
+    onward(2, 3)
+    arrive(weight.at[other], core_s.at[0], core_r.at[0])
+    onward(3, 0)
+    onward(3, 1)
+
+    @pl.when(apart != 0)
+    def _():
+        arrive(gain_tiles, gtz_s.at[0], gtz_r)
+
+    @pl.when(apart == 0)
+    def _():
         for one in outs_z:
             one.wait_send()
-
-    lands(2, 0)
-    onward(3, 0)
-
-    @pl.when(apart != 0)
-    def _():
-        arrive(gain_tiles, gtz_s.at[0], gtz_r)
 
     for yy in range(8):
         gain_rows[2 * yy : 2 * yy + 2, :] = gain_tiles[yy, 0:2, :]
@@ -359,7 +375,7 @@
 
         lax.fori_loop(low, high, one, 0)
 
-    block = weight[:, 0:96, :].reshape(192, BLOCK)
+    block = weight[...].reshape(192, BLOCK)
 
     def pre_act(n):
         low, size = SETS[n]
@@ -415,40 +431,48 @@
             total += jnp.sum(back * rows, axis=0, keepdims=True)
         return total
 
-    pairs(0, 8, 0, lambda e: (e % 4, e // 4))
+    def near(low, high):
+        pairs(low, high, 0, lambda e: (e % 4, e // 4))
+
+    def mid_a(low, high):
+        pairs(low, high, 16, lambda e: (4 + e % 3, e // 3))
+
+    def mid_b(low, high):
+        pairs(low, high, 28, lambda e: (e % 7, 4 + e // 7))
+
+    near(0, 4)
+    onward(3, 2)
+    near(4, 8)
+    onward(3, 3)
     pre_act(0)
-
-    lands(2, 1)
-    onward(3, 1)
-    lands(3, 0)
     onward(4, 0)
     sum_x(0)
-    lands(3, 1)
     onward(4, 1)
-
-    pairs(0, 6, 16, lambda e: (4 + e % 3, e // 3))
-    pairs(0, 10, 28, lambda e: (e % 7, 4 + e // 7))
+    mid_a(0, 3)
+    onward(4, 2)
+    mid_a(3, 6)
+    onward(4, 3)
+    mid_b(0, 10)
     pre_act(1)
     slope(0)
-
-    lands(4, 0)
-    lands(4, 1)
+    sum_x(1)
+    for h in range(4):
+        lands(4, h)
     pairs(0, 4, 48, lambda e: (e, 7))
     pairs(4, 8, 48, lambda e: (7 - e // 15, e - 8 - e // 15))
-    sum_x(1)
     pre_act(2)
     share(0)
     sum_x(2)
+    slope(1)
     shared(0)
     acc[...] = gradient(0)
-    slope(1)
     gain_sum = gain_part(0)
     slope(2)
     share(1)
-    share(2)
     shared(1)
     acc[...] += gradient(1)
     gain_sum += gain_part(1)
+    share(2)
     shared(2)
     rounded = (acc[...] + gradient(2)).astype(BF16)
 
@@ -571,8 +595,9 @@
             pltpu.VMEM((2, 32, BLOCK), BF16),
             pltpu.VMEM((2, 32, BLOCK), BF16),
             pltpu.VMEM((2, 32, BLOCK), BF16),
-            pltpu.VMEM((2, 112, BLOCK), BF16),
-            pltpu.VMEM((2, 112, BLOCK), BF16),
+            pltpu.VMEM((2, 96, BLOCK), BF16),
+            pltpu.VMEM((2, 96, BLOCK), BF16),
+            pltpu.VMEM((2, 8, LANES), F32),
             pltpu.VMEM((8, 8, A_ROWS, LANES), BF16),
             pltpu.VMEM((8, 8, B_ROWS, LANES), BF16),
             pltpu.VMEM((96, 512), F32),
@@ -595,9 +620,9 @@
             pltpu.VMEM((8, LANES), F32),
             dma((7,)), dma((7,)),
             dma((2,)), dma((2,)),
-            dma((2,)), dma((2,)),
+            dma((3,)), dma((3,)),
             dma((2, 7)), dma((2, 7)),
-            dma((4, 2, 4)), dma((4, 2, 4)),
+            dma((4, 4, 4)), dma((4, 4, 4)),
             dma((3,)), dma((3,)),
             dma((3, 3)), dma((3, 3)),
             dma((3, 3)), dma((3, 3)),
@@ -610,7 +635,7 @@
             dma((7,)), dma,
         ],
         compiler_params=pltpu.CompilerParams(
-            collective_id=0, has_side_effects=True, vmem_limit_bytes=56 * 2**20
+            collective_id=0, has_side_effects=True, vmem_limit_bytes=40 * 2**20
         ),
     )(tokens, slots, offsets, act_cot[0].T, jnp.asarray(away), pick, mask)
     return out.reshape(-1)[:SHARD]

time: 95.4 us -> 83.2 us (0.87)
  Pallas kernels: 89.2 us -> 79.4 us
  local copies, waits for them, and re-layouts: 6.03 us -> 3.23 us
    pallas_call x1, Pallas kernels: 89.2 us -> 79.4 us  [body(): pl.pallas_call(main_kernel, out_shape=jax.ShapeDtypeStruct((4616, LANES),...]
    unnamed x1 -> x13, local copies, waits for them, and re-layouts: 3.23 us -> 1.58 us
    reshape x1, local copies, waits for them, and re-layouts: 2.8 us -> 1.65 us  [body(): jnp.pad(old_slots, (0, LINES * LANES - old_slots.shape[0]))]
where the time goes in v3:
time: 83.2 us; the launch traced here: 82.7 us
  Pallas kernels  79.4 us (95%)
  local copies, waits for them, and re-layouts  3.23 us (4%)
    pallas_call x1, Pallas kernels, body(): pl.pallas_call(main_kernel, out_shape=jax.ShapeDtypeStruct((4616, LANES),...  79.4 us

profile of v3, /device:TPU:1, one launch (start us, length us, event | category | flops | bytes accessed | tf_op | source)
XLA Modules:
  0.0 82.7 jit_solution(8992474256219142245)
XLA Ops:
  0.0 0.0 copy-start
  0.0 0.0 copy-start.3
  0.0 0.0 copy-start.4
  0.0 0.0 copy-start.5
  0.0 0.0 copy-start.1
  0.0 0.0 copy-start.2
  0.0 1.7 %pad_bitcast_fusion.slots_ref = bf16[6928,128]{1,0:T(8,128)(2,1)S(1)} fusion(bf16[884808]{0:T(1024)(128)(2,1)} %param.9), kind=kLoop, calls=%fused_computation | loop fusion | bytes 3543184 | tf_op jit(solution)/shard_map/reshape | solution.py:575
  1.7 0.0 copy-done
  1.7 0.0 copy-done.3
  1.7 0.0 copy-done.4
  1.7 0.0 copy-done.5
  1.7 0.0 copy-done.1
  1.7 0.0 copy-done.2
  1.8 79.4 %shard_map.73 = f32[4616,128]{1,0:T(8,128)S(1)} custom-call(bf16[1,4,6144]{2,1,0:T(4,128)(2,1)S(1)} %copy-done.2, bf16[6928,128]{1,0:T(8,128)(2,1)S(1)} %pad_bitcast_fusion.slots_ref, s32[129]{0:T(256)S(1)} %copy-done.5, bf16[96,512]{1,0:T(8,128)(2,1)S(1)} %bitcast.8, s32[2,512]{1,0:T(2,128)S(1)} %copy-done.4, bf16[128,768]{1,0:T(8,128)(2,1)S(1)} %copy-done, ...), custom_call_target="tpu_custom_call" | custom-call | tf_op jit(solution)/shard_map/pallas_call | solution.py:582
  81.2 1.6 %copy.9 = f32[589872]{0:T(1024)} copy(f32[589872]{0:T(1024)S(1)} %bitcast.7) | data formatting | bytes 4718976
Async XLA Ops:
  0.0 1.7 %copy-start = (bf16[128,768]{1,0:T(8,128)(2,1)S(1)}, bf16[128,768]{1,0:T(8,128)(2,1)}, u32[]{:S(2)}) copy-start(bf16[128,768]{1,0:T(8,128)(2,1)} %constant.9.clone.pick_ref) | copy-start | bytes 589828
  0.0 1.7 %copy-start.3 = (f32[16,768]{1,0:T(8,128)S(1)}, f32[16,768]{1,0:T(8,128)}, u32[]{:S(2)}) copy-start(f32[16,768]{1,0:T(8,128)} %constant.10.clone.mask_ref) | copy-start | bytes 147460
  0.0 1.7 %copy-start.4 = (s32[2,512]{1,0:T(2,128)S(1)}, s32[2,512]{1,0:T(2,128)}, u32[]{:S(2)}) copy-start(s32[2,512]{1,0:T(2,128)} %constant.11.clone.away_ref) | copy-start | bytes 12292
  0.0 1.7 %copy-start.5 = (s32[129]{0:T(256)S(1)}, s32[129]{0:T(256)}, u32[]{:S(2)}) copy-start(s32[129]{0:T(256)} %off_ref.1) | copy-start | bytes 1552
  0.0 1.7 %copy-start.1 = (bf16[1,512,96]{1,2,0:T(8,128)(2,1)S(1)}, bf16[1,512,96]{1,2,0:T(8,128)(2,1)}, u32[]{:S(2)}) copy-start(bf16[1,512,96]{1,2,0:T(8,128)(2,1)} %param.8) | copy-start | bytes 294916
  0.0 1.7 %copy-start.2 = (bf16[1,4,6144]{2,1,0:T(4,128)(2,1)S(1)}, bf16[1,4,6144]{2,1,0:T(4,128)(2,1)}, u32[]{:S(2)}) copy-start(bf16[1,4,6144]{2,1,0:T(4,128)(2,1)} %tok_ref.1) | copy-start | bytes 147460

commit v4 on v3

--- a/solution.py
+++ b/solution.py
@@ -11,8 +11,8 @@
 SHARD = 589872
 EPSILON = 1e-06
 LINES = 6928
-FRONT = 2704
-BACK = 384
+FRONT = 2320
+BACK = 64
 BLOCK = 768
 LANES = 128
 A_ROWS = 112
@@ -22,14 +22,32 @@
 AWAY = (0, 1, -1, 2, -2, 3, -3, 4)
 SLOT = {d: n for n, d in enumerate(AWAY)}
 SLOT[-4] = SLOT[4]
-SETS = ((0, 128), (128, 256), (384, 128))
+SETS = 4
+SIZE = 128
 
 
 def chips_in_order():
-    near = [(a, b) for b in range(4) for a in range(4)]
-    mid = [(4 + e % 3, e // 3) for e in range(12)] + [(e % 7, 4 + e // 7) for e in range(20)]
-    far = [(e, 7) for e in range(8)] + [(7 - e // 15, e - 8 - e // 15) for e in range(8, 16)]
-    return near + mid + far
+    return [place(e) for place in (near, side, corner, far) for e in range(16)]
+
+
+def near(e):
+    return e % 4, e // 4
+
+
+def side(e):
+    beyond = e // 12
+    return (1 - beyond) * (4 + e % 3) + beyond * (e - 12), (1 - beyond) * (e // 3) + beyond * 4
+
+
+def corner(e):
+    beyond = e // 8
+    return (1 - beyond) * (e % 4) + beyond * (4 + (e - 8) % 3), (1 - beyond) * (5 + e // 4) + beyond * (4 + (e - 8) // 3)
+
+
+def far(e):
+    beyond = e // 8
+    last = e // 15
+    return (1 - beyond) * e + beyond * (7 - last), (1 - beyond) * 7 + beyond * (e - 8 - last)
 
 
 def lane_iota(rows):
@@ -53,18 +71,12 @@
     tok_ref, slots_ref, off_ref, cot_ref, away_ref, pick_ref, mask_ref, out_ref,
     wide, lines, packed, letters, mail, own, right_out, left_out, edge_right, edge_left,
     spill, weight, gain_pair, gath_a, gath_b, cot, norm, scaled,
-    part_1, part_2, part_3, part_in_1, part_in_2, part_in_3,
-    sums_1, sums_2, sums_3, sums_in_1, sums_in_2, sums_in_3, grads_1, grads_2, grads_3,
-    acc, result, block_out, gain_own, gain_tiles, gain_rows, gain_mine, gain_z, gain_y, gain_out,
+    part, part_in, sums, sums_in, grads,
+    acc, result, block_out, gain_own, gain_left, gain_right, gain_tiles, gain_rows, gain_mine, gain_z, gain_y, gain_out,
     mail_s, mail_r, edge_s, edge_r, core_s, core_r, one_s, one_r, two_s, two_r,
-    half_s, half_r, sum_s, sum_r, pg_s, pg_r, pgc_s, pgc_r, res_s, res_r,
+    half_s, half_r, sum_s, sum_r, pg_s, pg_r, pgc_s, pgc_r, last_s, last_r, direct_s, direct_r, res_s, res_r,
     gty_s, gty_r, gtz_s, gtz_r, gz_s, gz_r, gy_s, gy_r, gf_s, gf_r,
 ):
-    part = (part_1, part_2, part_3)
-    part_in = (part_in_1, part_in_2, part_in_3)
-    sums = (sums_1, sums_2, sums_3)
-    sums_in = (sums_in_1, sums_in_2, sums_in_3)
-    grads = (grads_1, grads_2, grads_3)
     x = lax.axis_index("dp")
     f = lax.axis_index("fsdp")
     c = f % 2
@@ -153,47 +165,58 @@
     shift_right = shift_own + SHARD
     shift_left = shift_own - SHARD
 
+    line16 = lax.broadcasted_iota(jnp.int32, (16, LANES), 0) * LANES + lane_iota(16)
+
     def widen(i, carry):
         rows = pl.ds(pl.multiple_of(i * 16, 16), 16)
-        wide[pl.ds(pl.multiple_of(FRONT + i * 16, 16), 16), :] = slots_ref[rows, :].astype(F32)
+        valid = line16 < length - i * (16 * LANES)
+        wide[pl.ds(pl.multiple_of(FRONT + i * 16, 16), 16), :] = jnp.where(valid, slots_ref[rows, :].astype(F32), 0.0)
         return carry
 
+    wide[0:FRONT, :] = jnp.zeros((FRONT, LANES), F32)
+    wide[FRONT + LINES :, :] = jnp.zeros((BACK, LANES), F32)
     lax.fori_loop(0, LINES // 16, widen, 0, unroll=8)
 
-    def extract(first, shift, rows):
-        turn = shift & (LANES - 1)
+    def turned(first, shift, rows):
         row = FRONT + first + lax.shift_right_arithmetic(shift, 7)
-        row = jnp.clip(row, 0, FRONT + LINES + BACK - rows - 1)
-        here = wide[pl.ds(row, rows), :]
-        after = wide[pl.ds(row + 1, rows), :]
-        back = (LANES - turn) & (LANES - 1)
-        lane = lane_iota(rows)
-        line = lax.broadcasted_iota(jnp.int32, (rows, LANES), 0)
-        moved = jnp.where(lane < LANES - turn, pltpu.roll(here, back, 1), pltpu.roll(after, back, 1))
-        slot = (first + line) * LANES + lane + shift
-        return jnp.where((slot >= 0) & (slot < length), moved, 0.0)
+        row = jnp.clip(row, 0, FRONT + LINES + BACK - rows)
+        back = (LANES - (shift & (LANES - 1))) & (LANES - 1)
+        return pltpu.roll(wide[pl.ds(row, rows), :], back, 1)
+
+    def before_cut(rows, shift):
+        return lane_iota(rows) < LANES - (shift & (LANES - 1))
+
+    def line_of(shift):
+        got = turned(0, shift, 8)
+        return jnp.where(before_cut(1, shift), got[0:1], got[1:2])
 
     def move(first_row, low, high, shift):
         def one(h, carry):
-            got = extract((first_row + h) * 48 + 12 * x, shift, 16)
-            lines[pl.ds(pl.multiple_of(h * 16, 16), 16), :] = got
+            lines[pl.ds(pl.multiple_of(h * 16, 16), 16), :] = turned((first_row + h) * 48 + 12 * x, shift, 16)
             return carry
 
-        lax.fori_loop(low, high, one, 0, unroll=4)
-
-    def keep(piece_ref, rows):
+        lax.fori_loop(low, high, one, 0, unroll=8)
+
+    def keep(piece_ref, rows, shift):
+        mask = before_cut(rows, shift)
+        here = lines[pl.ds(0, rows, stride=16), :]
         for k in range(12):
-            col = lines[pl.ds(k, rows, stride=16), :]
-            piece_ref[k // 6, :, (k % 6) * LANES : (k % 6 + 1) * LANES] = col.astype(BF16)
-
-    move(64, 0, 32, shift_left)
-    lines[0:1, :] = extract(0, shift_left + HID_DEV * D - 16, 8)[0:1]
-    keep(left_out, 32)
+            after = lines[pl.ds(k + 1, rows, stride=16), :]
+            piece_ref[k // 6, :, (k % 6) * LANES : (k % 6 + 1) * LANES] = jnp.where(mask, here, after).astype(BF16)
+            here = after
+
+    gain_row = jnp.broadcast_to(line_of(shift_left + HID_DEV * D - 16), (8, LANES))
+    gain_left[...] = gain_row
+    send(gain_left, gain_right, core_s.at[3], core_r.at[3], left)
+    gain_own[...] = jnp.broadcast_to(line_of(shift_own + HID_DEV * D - 16), (8, LANES))
+    lines[0:128, :] = jnp.zeros((128, LANES), F32)
+    move(64, 8, 32, shift_left)
+    keep(left_out, 32, shift_left)
     send(left_out, edge_left, edge_s.at[1], edge_r.at[1], left)
-    move(0, 0, 32, shift_right)
-    keep(right_out, 32)
+    move(0, 0, 25, shift_right)
+    lines[400:512, :] = jnp.zeros((112, LANES), F32)
+    keep(right_out, 32, shift_right)
     send(right_out, edge_right, edge_s.at[0], edge_r.at[0], right)
-    gain_own[...] = extract(0, shift_own + HID_DEV * D - 16, 8)
 
     for r in range(1, 8):
         arrive(mail.at[(g - r + 8) % 8], mail_s.at[r - 1], mail_r.at[r - 1])
@@ -219,25 +242,14 @@
         send(gath_a.at[0, 0], gath_a.at[n, 0], one_s.at[0, n - 1], one_r.at[0, n - 1], dev_u(d))
         send(gath_b.at[0, 0], gath_b.at[0, n], one_s.at[1, n - 1], one_r.at[1, n - 1], dev_v(d))
 
-    move(0, 0, 32, shift_own)
-    arrive(edge_left, edge_s.at[1], edge_r.at[1])
+    move(0, 0, 96, shift_own)
+    keep(own, 96, shift_own)
+    arrive(gain_right, core_s.at[3], core_r.at[3])
     lane8 = lane_iota(8)
-    gain_row = edge_left[0, 0:16, 0:LANES].astype(F32)[0:8] + gain_own[...]
-    gain_pair[pl.ds(c, 1)] = jnp.where((lane8 >= 16) & (lane8 < 64), gain_row, 0.0)[None]
+    gain_row = jnp.where((lane8 >= 16) & (lane8 < 64), gain_right[...] + gain_own[...], 0.0)
+    gain_pair[pl.ds(c, 1)] = gain_row[None]
     send(gain_pair.at[c], gain_pair.at[c], core_s.at[2], core_r.at[2], core)
-    move(0, 32, 64, shift_own)
-    arrive(gain_pair.at[other], core_s.at[2], core_r.at[2])
     apart = (z - g + 8) % 8
-    outs = [
-        copy(gain_tiles.at[y], gain_tiles.at[y], gty_s.at[r - 1], gty_r.at[r - 1], dev_y(r)) for r in range(1, 8)
-    ]
-
-    @pl.when(apart == 0)
-    def _():
-        rows = jnp.concatenate([gain_pair[0, 0:1], gain_pair[1, 0:1], jnp.zeros((6, LANES), F32)], axis=0)
-        gain_tiles[pl.ds(y, 1)] = rows[None]
-        for one in outs:
-            one.start()
 
     def unit_a(h, n):
         return gath_a.at[2 * h : 2 * h + 2, n]
@@ -268,10 +280,21 @@
 
     first_axis(1)
     onward(1, 0)
+    arrive(gain_pair.at[other], core_s.at[2], core_r.at[2])
+    outs = [
+        copy(gain_tiles.at[y], gain_tiles.at[y], gty_s.at[r - 1], gty_r.at[r - 1], dev_y(r)) for r in range(1, 8)
+    ]
+
+    @pl.when(apart == 0)
+    def _():
+        rows = jnp.concatenate([gain_pair[0, 0:1], gain_pair[1, 0:1], jnp.zeros((6, LANES), F32)], axis=0)
+        gain_tiles[pl.ds(y, 1)] = rows[None]
+        for one in outs:
+            one.start()
+
     first_axis(2)
     first_axis(3)
     onward(1, 1)
-    move(0, 64, 96, shift_own)
     first_axis(4)
     first_axis(5)
     onward(1, 2)
@@ -279,14 +302,12 @@
     first_axis(7)
     onward(1, 3)
 
-    keep(own, 96)
+    arrive(edge_left, edge_s.at[1], edge_r.at[1])
     arrive(edge_right, edge_s.at[0], edge_r.at[0])
-    row32 = lax.broadcasted_iota(jnp.int32, (32, BLOCK), 0)
     for half in range(2):
         spill[half, 0:32, :] = own[half, 0:32, :] + edge_right[half]
         spill[half, 32:64, :] = own[half, 32:64, :]
-        low = jnp.where(row32 >= 8, edge_left[half].astype(F32), 0.0)
-        spill[half, 64:96, :] = (own[half, 64:96, :].astype(F32) + low).astype(BF16)
+        spill[half, 64:96, :] = own[half, 64:96, :] + edge_left[half]
     send(spill.at[other], weight.at[c], core_s.at[0], core_r.at[0], core)
     weight[pl.ds(c, 1)] = spill[pl.ds(c, 1)]
     onward(2, 0)
@@ -364,131 +385,148 @@
                     ],
                     axis=0,
                 )
-                rows = pl.ds(pl.multiple_of(512 * xx + 8 * first, 16), 16)
+                rows = pl.ds(512 * xx + 8 * first, 16)
                 norm[rows, k * LANES : (k + 1) * LANES] = both
                 scaled[rows, k * LANES : (k + 1) * LANES] = (both * gain_k).astype(BF16)
 
-    def pairs(low, high, first, place):
-        def one(p, carry):
-            normalize(first + 2 * p, (place(2 * p), place(2 * p + 1)))
-            return carry
-
-        lax.fori_loop(low, high, one, 0)
+    def pairs(n, place, low=0, high=16):
+        for e in range(low, high, 2):
+            normalize(16 * n + e, (place(e), place(e + 1)))
 
     block = weight[...].reshape(192, BLOCK)
 
+    def rows_of(n, xx):
+        return slice(512 * xx + SIZE * n, 512 * xx + SIZE * (n + 1))
+
     def pre_act(n):
-        low, size = SETS[n]
         for xx in range(4):
             got = lax.dot_general(
-                block, scaled[512 * xx + low : 512 * xx + low + size, :], (((1,), (1,)), ((), ())),
-                preferred_element_type=F32,
+                block, scaled[rows_of(n, xx), :], (((1,), (1,)), ((), ())), preferred_element_type=F32
             )
-            part[n][0, xx] = got[0:96]
-            part[n][1, xx] = got[96:192]
-        send(part[n].at[other], part_in[n], half_s.at[n], half_r.at[n], core)
+            part[n, 0, xx] = got[0:96]
+            part[n, 1, xx] = got[96:192]
+        send(part.at[n, other], part_in.at[n], half_s.at[n], half_r.at[n], core)
 
     def sum_x(n):
-        arrive(part_in[n], half_s.at[n], half_r.at[n])
-        sums[n][...] = part[n][pl.ds(c, 1)][0] + part_in[n][...]
+        arrive(part_in.at[n], half_s.at[n], half_r.at[n])
+        sums[n] = part[n, pl.ds(c, 1)][0] + part_in[n]
         for r in range(1, 4):
-            send(sums[n].at[(x + r) % 4], sums_in[n].at[r - 1], sum_s.at[n, r - 1], sum_r.at[n, r - 1], dev_x(r))
+            send(sums.at[n, (x + r) % 4], sums_in.at[n, r - 1], sum_s.at[n, r - 1], sum_r.at[n, r - 1], dev_x(r))
+
+    def last_pre_act(n):
+        for r in (2, 1, 3, 0):
+            xx = (x + r) % 4
+            rows = scaled[pl.ds(pl.multiple_of(512 * xx + SIZE * n, SIZE), SIZE), :]
+            got = lax.dot_general(block, rows, (((1,), (1,)), ((), ())), preferred_element_type=F32)
+            part[n, 0, pl.ds(xx, 1)] = got[0:96][None]
+            part[n, 1, pl.ds(xx, 1)] = got[96:192][None]
+            send(part.at[n, other, xx], part_in.at[n, xx], last_s.at[r], last_r.at[r], core)
+
+    def last_sum_x(n):
+        for r in (2, 1, 3, 0):
+            xx = (x + r) % 4
+            arrive(part_in.at[n, xx], last_s.at[r], last_r.at[r])
+            sums[n, pl.ds(xx, 1)] = part[n, pl.ds(c, 1), pl.ds(xx, 1)][0] + part_in[n, pl.ds(xx, 1)]
+            if r:
+                send(sums.at[n, xx], sums_in.at[n, r - 1], sum_s.at[n, r - 1], sum_r.at[n, r - 1], dev_x(r))
 
     mine = pl.ds(pl.multiple_of(96 * c, 32), 96)
     theirs = pl.ds(pl.multiple_of(96 * other, 32), 96)
 
     def slope(n):
-        low, size = SETS[n]
         for r in range(1, 4):
-            arrive(sums_in[n].at[r - 1], sum_s.at[n, r - 1], sum_r.at[n, r - 1])
-        total = (sums[n][pl.ds(x, 1)][0] + sums_in[n][0]) + (sums_in[n][1] + sums_in[n][2])
-        grads[n][pl.ds(x, 1), mine, :] = (cot[:, low : low + size] * gelu_slope(total)).astype(BF16)[None]
-        for r in range(1, 4):
-            send(grads[n].at[x, mine], grads[n].at[x, mine], pg_s.at[n, r - 1], pg_r.at[n, r - 1], dev_x(r))
+            arrive(sums_in.at[n, r - 1], sum_s.at[n, r - 1], sum_r.at[n, r - 1])
+        total = (sums[n, pl.ds(x, 1)][0] + sums_in[n, 0]) + (sums_in[n, 1] + sums_in[n, 2])
+        got = (cot[:, SIZE * n : SIZE * (n + 1)] * gelu_slope(total)).astype(BF16)
+        grads[n, pl.ds(x, 1), mine, :] = got[None]
+        if n == SETS - 1:
+            for r in (4, 5, 3, 2, 6, 1, 7):
+                send(grads.at[n, x, mine], grads.at[n, x, mine], direct_s.at[r - 1], direct_r.at[r - 1], mate((g + r) % 8))
+        else:
+            for r in range(1, 4):
+                send(grads.at[n, x, mine], grads.at[n, x, mine], pg_s.at[n, r - 1], pg_r.at[n, r - 1], dev_x(r))
+
+    def last_shared(n):
+        for r in range(1, 8):
+            gg = (g - r + 8) % 8
+            rows = pl.ds(pl.multiple_of(96 * (gg % 2), 32), 96)
+            arrive(grads.at[n, gg // 2, rows], direct_s.at[r - 1], direct_r.at[r - 1])
 
     def share(n):
         for r in range(1, 4):
-            arrive(grads[n].at[(x - r + 4) % 4, mine], pg_s.at[n, r - 1], pg_r.at[n, r - 1])
-        send(grads[n].at[:, mine], grads[n].at[:, mine], pgc_s.at[n], pgc_r.at[n], core)
+            arrive(grads.at[n, (x - r + 4) % 4, mine], pg_s.at[n, r - 1], pg_r.at[n, r - 1])
+        send(grads.at[n, :, mine], grads.at[n, :, mine], pgc_s.at[n], pgc_r.at[n], core)
 
     def shared(n):
-        arrive(grads[n].at[:, theirs], pgc_s.at[n], pgc_r.at[n])
+        arrive(grads.at[n, :, theirs], pgc_s.at[n], pgc_r.at[n])
 
     def gradient(n):
-        low, size = SETS[n]
         total = jnp.zeros((192, BLOCK), F32)
         for xx in range(4):
-            rows = scaled[512 * xx + low : 512 * xx + low + size, :]
-            total += jnp.dot(grads[n][xx], rows, preferred_element_type=F32)
+            total += jnp.dot(grads[n, xx], scaled[rows_of(n, xx), :], preferred_element_type=F32)
         return total
 
     def gain_part(n):
-        low, size = SETS[n]
         total = jnp.zeros((1, BLOCK), F32)
         for xx in range(4):
-            back = lax.dot_general(grads[n][xx], block, (((0,), (0,)), ((), ())), preferred_element_type=F32)
-            rows = norm[512 * xx + low : 512 * xx + low + size, :]
-            total += jnp.sum(back * rows, axis=0, keepdims=True)
+            back = lax.dot_general(grads[n, xx], block, (((0,), (0,)), ((), ())), preferred_element_type=F32)
+            total += jnp.sum(back * norm[rows_of(n, xx), :], axis=0, keepdims=True)
         return total
 
-    def near(low, high):
-        pairs(low, high, 0, lambda e: (e % 4, e // 4))
-
-    def mid_a(low, high):
-        pairs(low, high, 16, lambda e: (4 + e % 3, e // 3))
-
-    def mid_b(low, high):
-        pairs(low, high, 28, lambda e: (e % 7, 4 + e // 7))
-
-    near(0, 4)
+    pairs(0, near)
+    pre_act(0)
     onward(3, 2)
-    near(4, 8)
+    sum_x(0)
     onward(3, 3)
-    pre_act(0)
     onward(4, 0)
-    sum_x(0)
     onward(4, 1)
-    mid_a(0, 3)
+    pairs(1, side)
+    pre_act(1)
     onward(4, 2)
-    mid_a(3, 6)
+    sum_x(1)
+    pairs(2, corner, 0, 8)
     onward(4, 3)
-    mid_b(0, 10)
-    pre_act(1)
+    pairs(2, corner, 8, 16)
+    pre_act(2)
+    sum_x(2)
     slope(0)
-    sum_x(1)
     for h in range(4):
         lands(4, h)
-    pairs(0, 4, 48, lambda e: (e, 7))
-    pairs(4, 8, 48, lambda e: (7 - e // 15, e - 8 - e // 15))
-    pre_act(2)
+    pairs(3, far)
+    last_pre_act(3)
+    last_sum_x(3)
+    slope(1)
     share(0)
-    sum_x(2)
-    slope(1)
     shared(0)
     acc[...] = gradient(0)
     gain_sum = gain_part(0)
     slope(2)
     share(1)
+    slope(3)
     shared(1)
     acc[...] += gradient(1)
     gain_sum += gain_part(1)
     share(2)
     shared(2)
-    rounded = (acc[...] + gradient(2)).astype(BF16)
+    acc[...] += gradient(2)
+    gain_sum += gain_part(2)
+    last_shared(3)
+    rounded = (acc[...] + gradient(3)).astype(BF16)
 
     block_out[0] = rounded[0:96]
     block_out[1] = rounded[96:192]
     send(block_out.at[other], result.at[x, c], core_s.at[1], core_r.at[1], core)
     result[pl.ds(x, 1), pl.ds(c, 1)] = block_out[pl.ds(c, 1)][None]
-    for m, d in enumerate((1, -1)):
-        send(result.at[x, c], result.at[x, c], res_s.at[m, 0], res_r.at[m, 0], dev_x(d))
-    gain_sum += gain_part(2)
+    way = 1 - 2 * c
+    send(result.at[x, c], result.at[x, c], res_s.at[c, 0], res_r.at[c, 0], dev_x(way))
+    arrive(result.at[x, other], core_s.at[1], core_r.at[1])
+    send(result.at[x, other], result.at[x, other], res_s.at[other, 0], res_r.at[other, 0], dev_x(-way))
+    send(result.at[x, other], result.at[x, other], res_s.at[c, 1], res_r.at[c, 1], dev_x(way))
+    send(result.at[x, c], result.at[x, c], res_s.at[other, 1], res_r.at[other, 1], dev_x(-way))
+    gain_sum += gain_part(3)
     for k in range(6):
         gain_mine[k : k + 1, :] = gain_sum[:, k * LANES : (k + 1) * LANES]
     gain_mine[6:8, :] = jnp.zeros((2, LANES), F32)
-    arrive(result.at[x, other], core_s.at[1], core_r.at[1])
-    for m, d in enumerate((1, -1)):
-        send(result.at[x, other], result.at[x, other], res_s.at[m, 1], res_r.at[m, 1], dev_x(d))
 
     to_z = copy(gain_mine, gain_z.at[(apart + 7) % 8], gz_s, gz_r.at[(apart + 7) % 8], at(x, g * 16 + y * 2 + c))
 
@@ -516,12 +554,9 @@
         for one in outs_y:
             one.start()
 
-    arrive(result.at[(x + 3) % 4, c], res_s.at[0, 0], res_r.at[0, 0])
-    arrive(result.at[(x + 1) % 4, c], res_s.at[1, 0], res_r.at[1, 0])
-    arrive(result.at[(x + 3) % 4, other], res_s.at[0, 1], res_r.at[0, 1])
-    send(result.at[(x + 3) % 4, 0], result.at[(x + 3) % 4, 0], res_s.at[0, 2], res_r.at[0, 2], dev_x(1))
-    arrive(result.at[(x + 1) % 4, other], res_s.at[1, 1], res_r.at[1, 1])
-    send(result.at[(x + 1) % 4, 1], result.at[(x + 1) % 4, 1], res_s.at[1, 2], res_r.at[1, 2], dev_x(-1))
+    for m, d in enumerate((1, -1)):
+        arrive(result.at[(x - d + 4) % 4, m], res_s.at[m, 0], res_r.at[m, 0])
+        send(result.at[(x - d + 4) % 4, m], result.at[(x - d + 4) % 4, m], res_s.at[m, 2], res_r.at[m, 2], dev_x(d))
 
     outs_f = [copy(gain_out, gain_out, gf_s.at[r - 1], gf_r, mate((g + r) % 8)) for r in range(1, 8)]
 
@@ -535,9 +570,11 @@
         for one in outs_f:
             one.start()
 
-    for half in range(2):
-        spell((x + 3) % 4, half)
-        spell((x + 1) % 4, half)
+    for m, d in enumerate((1, -1)):
+        spell((x - d + 4) % 4, m)
+    for m, d in enumerate((1, -1)):
+        arrive(result.at[(x - d + 4) % 4, 1 - m], res_s.at[m, 1], res_r.at[m, 1])
+        spell((x - d + 4) % 4, 1 - m)
 
     @pl.when(apart != 0)
     def _():
@@ -603,14 +640,16 @@
             pltpu.VMEM((96, 512), F32),
             pltpu.VMEM((2048, BLOCK), F32),
             pltpu.VMEM((2048, BLOCK), BF16),
-            *[pltpu.VMEM((2, 4, 96, size), F32) for _, size in SETS],
-            *[pltpu.VMEM((4, 96, size), F32) for _, size in SETS],
-            *[pltpu.VMEM((4, 96, size), F32) for _, size in SETS],
-            *[pltpu.VMEM((3, 96, size), F32) for _, size in SETS],
-            *[pltpu.VMEM((4, 192, size), BF16) for _, size in SETS],
+            pltpu.VMEM((SETS, 2, 4, 96, SIZE), F32),
+            pltpu.VMEM((SETS, 4, 96, SIZE), F32),
+            pltpu.VMEM((SETS, 4, 96, SIZE), F32),
+            pltpu.VMEM((SETS, 3, 96, SIZE), F32),
+            pltpu.VMEM((SETS, 4, 192, SIZE), BF16),
             pltpu.VMEM((192, BLOCK), F32),
             pltpu.VMEM((4, 2, 96, BLOCK), BF16),
             pltpu.VMEM((2, 96, BLOCK), BF16),
+            pltpu.VMEM((8, LANES), F32),
+            pltpu.VMEM((8, LANES), F32),
             pltpu.VMEM((8, LANES), F32),
             pltpu.VMEM((8, 8, LANES), F32),
             pltpu.VMEM((16, LANES), F32),
@@ -620,13 +659,15 @@
             pltpu.VMEM((8, LANES), F32),
             dma((7,)), dma((7,)),
             dma((2,)), dma((2,)),
-            dma((3,)), dma((3,)),
+            dma((4,)), dma((4,)),
             dma((2, 7)), dma((2, 7)),
             dma((4, 4, 4)), dma((4, 4, 4)),
-            dma((3,)), dma((3,)),
-            dma((3, 3)), dma((3, 3)),
-            dma((3, 3)), dma((3, 3)),
-            dma((3,)), dma((3,)),
+            dma((SETS,)), dma((SETS,)),
+            dma((SETS, 3)), dma((SETS, 3)),
+            dma((SETS, 3)), dma((SETS, 3)),
+            dma((SETS,)), dma((SETS,)),
+            dma((4,)), dma((4,)),
+            dma((7,)), dma((7,)),
             dma((2, 3)), dma((2, 3)),
             dma((7,)), dma((7,)),
             dma((7,)), dma,

time: 83.2 us -> 80 us (0.962)
  Pallas kernels: 79.4 us -> 76.6 us
    pallas_call x1, Pallas kernels: 79.4 us -> 76.6 us  [body(): pl.pallas_call(main_kernel, out_shape=jax.ShapeDtypeStruct((4616, LANES),...]
where the time goes in v4:
time: 80 us; the launch traced here: 79.9 us
  Pallas kernels  76.6 us (96%)
  local copies, waits for them, and re-layouts  3.23 us (4%)
    pallas_call x1, Pallas kernels, body(): pl.pallas_call(main_kernel, out_shape=jax.ShapeDtypeStruct((4616, LANES),...  76.6 us
    reshape x1, local copies, waits for them, and re-layouts, body(): jnp.pad(old_slots, (0, LINES * LANES - old_slots.shape[0]))  1.65 us

profile of v4, /device:TPU:1, one launch (start us, length us, event | category | flops | bytes accessed | tf_op | source)
XLA Modules:
  0.0 79.9 jit_solution(12572964647588421181)
XLA Ops:
  0.0 0.0 copy-start
  0.0 0.0 copy-start.3
  0.0 0.0 copy-start.4
  0.0 0.0 copy-start.5
  0.0 0.0 copy-start.1
  0.0 0.0 copy-start.2
  0.0 1.7 %pad_bitcast_fusion.slots_ref = bf16[6928,128]{1,0:T(8,128)(2,1)S(1)} fusion(bf16[884808]{0:T(1024)(128)(2,1)} %param.9), kind=kLoop, calls=%fused_computation | loop fusion | bytes 3543184 | tf_op jit(solution)/shard_map/reshape | solution.py:612
  1.7 0.0 copy-done
  1.7 0.0 copy-done.3
  1.7 0.0 copy-done.4
  1.7 0.0 copy-done.5
  1.7 0.0 copy-done.1
  1.7 0.0 copy-done.2
  1.8 76.6 %shard_map.73 = f32[4616,128]{1,0:T(8,128)S(1)} custom-call(bf16[1,4,6144]{2,1,0:T(4,128)(2,1)S(1)} %copy-done.2, bf16[6928,128]{1,0:T(8,128)(2,1)S(1)} %pad_bitcast_fusion.slots_ref, s32[129]{0:T(256)S(1)} %copy-done.5, bf16[96,512]{1,0:T(8,128)(2,1)S(1)} %bitcast.8, s32[2,512]{1,0:T(2,128)S(1)} %copy-done.4, bf16[128,768]{1,0:T(8,128)(2,1)S(1)} %copy-done, ...), custom_call_target="tpu_custom_call" | custom-call | tf_op jit(solution)/shard_map/pallas_call | solution.py:619
  78.3 1.6 %copy.9 = f32[589872]{0:T(1024)} copy(f32[589872]{0:T(1024)S(1)} %bitcast.7) | data formatting | bytes 4718976
Async XLA Ops:
  0.0 1.7 %copy-start = (bf16[128,768]{1,0:T(8,128)(2,1)S(1)}, bf16[128,768]{1,0:T(8,128)(2,1)}, u32[]{:S(2)}) copy-start(bf16[128,768]{1,0:T(8,128)(2,1)} %constant.9.clone.pick_ref) | copy-start | bytes 589828
  0.0 1.7 %copy-start.3 = (f32[16,768]{1,0:T(8,128)S(1)}, f32[16,768]{1,0:T(8,128)}, u32[]{:S(2)}) copy-start(f32[16,768]{1,0:T(8,128)} %constant.10.clone.mask_ref) | copy-start | bytes 147460
  0.0 1.7 %copy-start.4 = (s32[2,512]{1,0:T(2,128)S(1)}, s32[2,512]{1,0:T(2,128)}, u32[]{:S(2)}) copy-start(s32[2,512]{1,0:T(2,128)} %constant.11.clone.away_ref) | copy-start | bytes 12292
  0.0 1.7 %copy-start.5 = (s32[129]{0:T(256)S(1)}, s32[129]{0:T(256)}, u32[]{:S(2)}) copy-start(s32[129]{0:T(256)} %off_ref.1) | copy-start | bytes 1552
  0.0 1.7 %copy-start.1 = (bf16[1,512,96]{1,2,0:T(8,128)(2,1)S(1)}, bf16[1,512,96]{1,2,0:T(8,128)(2,1)}, u32[]{:S(2)}) copy-start(bf16[1,512,96]{1,2,0:T(8,128)(2,1)} %param.8) | copy-start | bytes 294916
  0.0 1.7 %copy-start.2 = (bf16[1,4,6144]{2,1,0:T(4,128)(2,1)S(1)}, bf16[1,4,6144]{2,1,0:T(4,128)(2,1)}, u32[]{:S(2)}) copy-start(bf16[1,4,6144]{2,1,0:T(4,128)(2,1)} %tok_ref.1) | copy-start | bytes 147460

commit v5 on v4

--- a/solution.py
+++ b/solution.py
@@ -265,9 +265,9 @@
                 arrive(unit(h, SLOT[-d * s]), two_s.at[n, h, s - 1], two_r.at[n, h, s - 1])
 
     def onward(s, h):
-        if s > 1:
-            lands(s - 1, h)
         for n, (unit, dev, d) in enumerate(streams):
+            if s > 1:
+                arrive(unit(h, SLOT[-d * (s - 1)]), two_s.at[n, h, s - 2], two_r.at[n, h, s - 2])
             if s < 4 or (h < 2) == (d == 1):
                 send(
                     unit(h, SLOT[-d * (s - 1)]), unit(h, SLOT[-d * s]),
@@ -502,6 +502,8 @@
     gain_sum = gain_part(0)
     slope(2)
     share(1)
+    early = list(sends)
+    sends.clear()
     slope(3)
     shared(1)
     acc[...] += gradient(1)
@@ -510,7 +512,20 @@
     shared(2)
     acc[...] += gradient(2)
     gain_sum += gain_part(2)
+    for one in early:
+        one.wait_send()
     last_shared(3)
+    gain_sum += gain_part(3)
+    for k in range(6):
+        gain_mine[k : k + 1, :] = gain_sum[:, k * LANES : (k + 1) * LANES]
+    gain_mine[6:8, :] = jnp.zeros((2, LANES), F32)
+
+    to_z = copy(gain_mine, gain_z.at[(apart + 7) % 8], gz_s, gz_r.at[(apart + 7) % 8], at(x, g * 16 + y * 2 + c))
+
+    @pl.when(apart != 0)
+    def _():
+        to_z.start()
+
     rounded = (acc[...] + gradient(3)).astype(BF16)
 
     block_out[0] = rounded[0:96]
@@ -523,16 +538,6 @@
     send(result.at[x, other], result.at[x, other], res_s.at[other, 0], res_r.at[other, 0], dev_x(-way))
     send(result.at[x, other], result.at[x, other], res_s.at[c, 1], res_r.at[c, 1], dev_x(way))
     send(result.at[x, c], result.at[x, c], res_s.at[other, 1], res_r.at[other, 1], dev_x(-way))
-    gain_sum += gain_part(3)
-    for k in range(6):
-        gain_mine[k : k + 1, :] = gain_sum[:, k * LANES : (k + 1) * LANES]
-    gain_mine[6:8, :] = jnp.zeros((2, LANES), F32)
-
-    to_z = copy(gain_mine, gain_z.at[(apart + 7) % 8], gz_s, gz_r.at[(apart + 7) % 8], at(x, g * 16 + y * 2 + c))
-
-    @pl.when(apart != 0)
-    def _():
-        to_z.start()
 
     def spell(xx, half):
         for k in range(6):

time: 80 us -> 80.3 us (level)
  no operation moved by 1% of the time
where the time goes in v5:
time: 80.3 us; the launch traced here: 80.2 us
  Pallas kernels  76.9 us (96%)
  local copies, waits for them, and re-layouts  3.23 us (4%)
    pallas_call x1, Pallas kernels, body(): pl.pallas_call(main_kernel, out_shape=jax.ShapeDtypeStruct((4616, LANES),...  76.9 us
    reshape x1, local copies, waits for them, and re-layouts, body(): jnp.pad(old_slots, (0, LINES * LANES - old_slots.shape[0]))  1.65 us

profile of v5, /device:TPU:1, one launch (start us, length us, event | category | flops | bytes accessed | tf_op | source)
XLA Modules:
  0.0 80.2 jit_solution(688979593647715674)
XLA Ops:
  0.0 0.0 copy-start
  0.0 0.0 copy-start.3
  0.0 0.0 copy-start.4
  0.0 0.0 copy-start.5
  0.0 0.0 copy-start.1
  0.0 0.0 copy-start.2
  0.0 1.7 %pad_bitcast_fusion.slots_ref = bf16[6928,128]{1,0:T(8,128)(2,1)S(1)} fusion(bf16[884808]{0:T(1024)(128)(2,1)} %param.9), kind=kLoop, calls=%fused_computation | loop fusion | bytes 3543184 | tf_op jit(solution)/shard_map/reshape | solution.py:617
  1.7 0.0 copy-done
  1.7 0.0 copy-done.3
  1.7 0.0 copy-done.4
  1.7 0.0 copy-done.5
  1.7 0.0 copy-done.1
  1.7 0.0 copy-done.2
  1.8 76.9 %shard_map.73 = f32[4616,128]{1,0:T(8,128)S(1)} custom-call(bf16[1,4,6144]{2,1,0:T(4,128)(2,1)S(1)} %copy-done.2, bf16[6928,128]{1,0:T(8,128)(2,1)S(1)} %pad_bitcast_fusion.slots_ref, s32[129]{0:T(256)S(1)} %copy-done.5, bf16[96,512]{1,0:T(8,128)(2,1)S(1)} %bitcast.8, s32[2,512]{1,0:T(2,128)S(1)} %copy-done.4, bf16[128,768]{1,0:T(8,128)(2,1)S(1)} %copy-done, ...), custom_call_target="tpu_custom_call" | custom-call | tf_op jit(solution)/shard_map/pallas_call | solution.py:624
  78.6 1.6 %copy.9 = f32[589872]{0:T(1024)} copy(f32[589872]{0:T(1024)S(1)} %bitcast.7) | data formatting | bytes 4718976
Async XLA Ops:
  0.0 1.7 %copy-start = (bf16[128,768]{1,0:T(8,128)(2,1)S(1)}, bf16[128,768]{1,0:T(8,128)(2,1)}, u32[]{:S(2)}) copy-start(bf16[128,768]{1,0:T(8,128)(2,1)} %constant.9.clone.pick_ref) | copy-start | bytes 589828
  0.0 1.7 %copy-start.3 = (f32[16,768]{1,0:T(8,128)S(1)}, f32[16,768]{1,0:T(8,128)}, u32[]{:S(2)}) copy-start(f32[16,768]{1,0:T(8,128)} %constant.10.clone.mask_ref) | copy-start | bytes 147460
  0.0 1.7 %copy-start.4 = (s32[2,512]{1,0:T(2,128)S(1)}, s32[2,512]{1,0:T(2,128)}, u32[]{:S(2)}) copy-start(s32[2,512]{1,0:T(2,128)} %constant.11.clone.away_ref) | copy-start | bytes 12292
  0.0 1.7 %copy-start.5 = (s32[129]{0:T(256)S(1)}, s32[129]{0:T(256)}, u32[]{:S(2)}) copy-start(s32[129]{0:T(256)} %off_ref.1) | copy-start | bytes 1552
  0.0 1.7 %copy-start.1 = (bf16[1,512,96]{1,2,0:T(8,128)(2,1)S(1)}, bf16[1,512,96]{1,2,0:T(8,128)(2,1)}, u32[]{:S(2)}) copy-start(bf16[1,512,96]{1,2,0:T(8,128)(2,1)} %param.8) | copy-start | bytes 294916
  0.0 1.7 %copy-start.2 = (bf16[1,4,6144]{2,1,0:T(4,128)(2,1)S(1)}, bf16[1,4,6144]{2,1,0:T(4,128)(2,1)}, u32[]{:S(2)}) copy-start(bf16[1,4,6144]{2,1,0:T(4,128)(2,1)} %tok_ref.1) | copy-start | bytes 147460

commit v6 on v4

--- a/solution.py
+++ b/solution.py
@@ -410,7 +410,7 @@
     def sum_x(n):
         arrive(part_in.at[n], half_s.at[n], half_r.at[n])
         sums[n] = part[n, pl.ds(c, 1)][0] + part_in[n]
-        for r in range(1, 4):
+        for r in (2, 1, 3):
             send(sums.at[n, (x + r) % 4], sums_in.at[n, r - 1], sum_s.at[n, r - 1], sum_r.at[n, r - 1], dev_x(r))
 
     def last_pre_act(n):
@@ -443,7 +443,7 @@
             for r in (4, 5, 3, 2, 6, 1, 7):
                 send(grads.at[n, x, mine], grads.at[n, x, mine], direct_s.at[r - 1], direct_r.at[r - 1], mate((g + r) % 8))
         else:
-            for r in range(1, 4):
+            for r in (2, 1, 3):
                 send(grads.at[n, x, mine], grads.at[n, x, mine], pg_s.at[n, r - 1], pg_r.at[n, r - 1], dev_x(r))
 
     def last_shared(n):
@@ -502,6 +502,8 @@
     gain_sum = gain_part(0)
     slope(2)
     share(1)
+    done = list(sends)
+    sends.clear()
     slope(3)
     shared(1)
     acc[...] += gradient(1)
@@ -510,6 +512,8 @@
     shared(2)
     acc[...] += gradient(2)
     gain_sum += gain_part(2)
+    for one in done:
+        one.wait_send()
     last_shared(3)
     rounded = (acc[...] + gradient(3)).astype(BF16)
 
@@ -518,11 +522,17 @@
     send(block_out.at[other], result.at[x, c], core_s.at[1], core_r.at[1], core)
     result[pl.ds(x, 1), pl.ds(c, 1)] = block_out[pl.ds(c, 1)][None]
     way = 1 - 2 * c
-    send(result.at[x, c], result.at[x, c], res_s.at[c, 0], res_r.at[c, 0], dev_x(way))
+
+    def spread(xx, half, rows, m, k, d):
+        send(result.at[xx, half, rows], result.at[xx, half, rows], res_s.at[m, k], res_r.at[m, k], dev_x(d))
+
+    every, upper, lower = slice(0, 96), slice(0, 48), slice(48, 96)
+    spread(x, c, every, c, 0, way)
+    spread(x, c, upper, other, 3, -way)
     arrive(result.at[x, other], core_s.at[1], core_r.at[1])
-    send(result.at[x, other], result.at[x, other], res_s.at[other, 0], res_r.at[other, 0], dev_x(-way))
-    send(result.at[x, other], result.at[x, other], res_s.at[c, 1], res_r.at[c, 1], dev_x(way))
-    send(result.at[x, c], result.at[x, c], res_s.at[other, 1], res_r.at[other, 1], dev_x(-way))
+    spread(x, other, every, other, 0, -way)
+    spread(x, other, every, c, 1, way)
+    spread(x, c, lower, other, 1, -way)
     gain_sum += gain_part(3)
     for k in range(6):
         gain_mine[k : k + 1, :] = gain_sum[:, k * LANES : (k + 1) * LANES]
@@ -554,9 +564,15 @@
         for one in outs_y:
             one.start()
 
-    for m, d in enumerate((1, -1)):
-        arrive(result.at[(x - d + 4) % 4, m], res_s.at[m, 0], res_r.at[m, 0])
-        send(result.at[(x - d + 4) % 4, m], result.at[(x - d + 4) % 4, m], res_s.at[m, 2], res_r.at[m, 2], dev_x(d))
+    behind, ahead = (x - way + 4) % 4, (x + way + 4) % 4
+
+    def came(xx, half, rows, m, k):
+        arrive(result.at[xx, half, rows], res_s.at[m, k], res_r.at[m, k])
+
+    came(behind, c, every, c, 0)
+    spread(behind, c, every, c, 2, way)
+    came(ahead, other, every, other, 0)
+    spread(ahead, other, every, other, 2, -way)
 
     outs_f = [copy(gain_out, gain_out, gf_s.at[r - 1], gf_r, mate((g + r) % 8)) for r in range(1, 8)]
 
@@ -570,11 +586,13 @@
         for one in outs_f:
             one.start()
 
-    for m, d in enumerate((1, -1)):
-        spell((x - d + 4) % 4, m)
-    for m, d in enumerate((1, -1)):
-        arrive(result.at[(x - d + 4) % 4, 1 - m], res_s.at[m, 1], res_r.at[m, 1])
-        spell((x - d + 4) % 4, 1 - m)
+    spell(behind, c)
+    spell(ahead, other)
+    came(behind, other, every, c, 1)
+    spell(behind, other)
+    came(ahead, c, upper, other, 3)
+    came(ahead, c, lower, other, 1)
+    spell(ahead, c)
 
     @pl.when(apart != 0)
     def _():
@@ -668,7 +686,7 @@
             dma((SETS,)), dma((SETS,)),
             dma((4,)), dma((4,)),
             dma((7,)), dma((7,)),
-            dma((2, 3)), dma((2, 3)),
+            dma((2, 4)), dma((2, 4)),
             dma((7,)), dma((7,)),
             dma((7,)), dma,
             dma, dma((8,)),

time: 80 us -> 79.8 us (level)
  no operation moved by 1% of the time
where the time goes in v6:
time: 79.8 us; the launch traced here: 79.4 us
  Pallas kernels  76.1 us (95%)
  local copies, waits for them, and re-layouts  3.23 us (4%)
    pallas_call x1, Pallas kernels, body(): pl.pallas_call(main_kernel, out_shape=jax.ShapeDtypeStruct((4616, LANES),...  76.1 us
    reshape x1, local copies, waits for them, and re-layouts, body(): jnp.pad(old_slots, (0, LINES * LANES - old_slots.shape[0]))  1.65 us

profile of v6, /device:TPU:1, one launch (start us, length us, event | category | flops | bytes accessed | tf_op | source)
XLA Modules:
  0.0 79.4 jit_solution(14801220919957678891)
XLA Ops:
  0.0 0.0 copy-start
  0.0 0.0 copy-start.3
  0.0 0.0 copy-start.4
  0.0 0.0 copy-start.5
  0.0 0.0 copy-start.1
  0.0 0.0 copy-start.2
  0.0 1.7 %pad_bitcast_fusion.slots_ref = bf16[6928,128]{1,0:T(8,128)(2,1)S(1)} fusion(bf16[884808]{0:T(1024)(128)(2,1)} %param.9), kind=kLoop, calls=%fused_computation | loop fusion | bytes 3543184 | tf_op jit(solution)/shard_map/reshape | solution.py:630
  1.7 0.0 copy-done
  1.7 0.0 copy-done.3
  1.7 0.0 copy-done.4
  1.7 0.0 copy-done.5
  1.7 0.0 copy-done.1
  1.7 0.0 copy-done.2
  1.8 76.1 %shard_map.73 = f32[4616,128]{1,0:T(8,128)S(1)} custom-call(bf16[1,4,6144]{2,1,0:T(4,128)(2,1)S(1)} %copy-done.2, bf16[6928,128]{1,0:T(8,128)(2,1)S(1)} %pad_bitcast_fusion.slots_ref, s32[129]{0:T(256)S(1)} %copy-done.5, bf16[96,512]{1,0:T(8,128)(2,1)S(1)} %bitcast.8, s32[2,512]{1,0:T(2,128)S(1)} %copy-done.4, bf16[128,768]{1,0:T(8,128)(2,1)S(1)} %copy-done, ...), custom_call_target="tpu_custom_call" | custom-call | tf_op jit(solution)/shard_map/pallas_call | solution.py:637
  77.9 1.6 %copy.9 = f32[589872]{0:T(1024)} copy(f32[589872]{0:T(1024)S(1)} %bitcast.7) | data formatting | bytes 4718976
Async XLA Ops:
  0.0 1.7 %copy-start = (bf16[128,768]{1,0:T(8,128)(2,1)S(1)}, bf16[128,768]{1,0:T(8,128)(2,1)}, u32[]{:S(2)}) copy-start(bf16[128,768]{1,0:T(8,128)(2,1)} %constant.9.clone.pick_ref) | copy-start | bytes 589828
  0.0 1.7 %copy-start.3 = (f32[16,768]{1,0:T(8,128)S(1)}, f32[16,768]{1,0:T(8,128)}, u32[]{:S(2)}) copy-start(f32[16,768]{1,0:T(8,128)} %constant.10.clone.mask_ref) | copy-start | bytes 147460
  0.0 1.7 %copy-start.4 = (s32[2,512]{1,0:T(2,128)S(1)}, s32[2,512]{1,0:T(2,128)}, u32[]{:S(2)}) copy-start(s32[2,512]{1,0:T(2,128)} %constant.11.clone.away_ref) | copy-start | bytes 12292
  0.0 1.7 %copy-start.5 = (s32[129]{0:T(256)S(1)}, s32[129]{0:T(256)}, u32[]{:S(2)}) copy-start(s32[129]{0:T(256)} %off_ref.1) | copy-start | bytes 1552
  0.0 1.7 %copy-start.1 = (bf16[1,512,96]{1,2,0:T(8,128)(2,1)S(1)}, bf16[1,512,96]{1,2,0:T(8,128)(2,1)}, u32[]{:S(2)}) copy-start(bf16[1,512,96]{1,2,0:T(8,128)(2,1)} %param.8) | copy-start | bytes 294916
  0.0 1.7 %copy-start.2 = (bf16[1,4,6144]{2,1,0:T(4,128)(2,1)S(1)}, bf16[1,4,6144]{2,1,0:T(4,128)(2,1)}, u32[]{:S(2)}) copy-start(bf16[1,4,6144]{2,1,0:T(4,128)(2,1)} %tok_ref.1) | copy-start | bytes 147460
